TPU v7x, 32 devices: a whole 2x2x4 slice. The times are simulated.
32 devices in a mesh: dp: 8 (over z, x), seq: 4 (over y, core).
Axes of the slice: x: 2, y: 2, z: 4, core: 2. Of those that a mesh axis runs over, the one named last changes fastest.
Arguments:
- inputs: bfloat16 [8, 1024, 768], P('dp', 'seq'), may hold values from -6 to 6
- cotangent: bfloat16 [8, 1024, 768], P('dp', 'seq'), may hold values from -6 to 6
- image_lengths: int32 [8, 8], P('dp'), may hold values from 1 to 384, 1024 in all within a row
- attention_weight: float32 [2, 4, 768, 768], P(None, None, ('dp', 'seq')), may hold values from -1.299038 to 1.299038
- attention_moment: float32 [2, 4, 768, 768], P(None, None, ('dp', 'seq')), may hold values from -56 to 56
- attention_average: float32 [2, 4, 768, 768], P(None, None, ('dp', 'seq')), may hold values from -0.21875 to 0.21875
- up_weight: float32 [2, 768, 3072], P(None, ('dp', 'seq')), may hold values from -0.21875 to 0.21875
- up_moment: float32 [2, 768, 3072], P(None, ('dp', 'seq')), may hold values from -112 to 112
- up_average: float32 [2, 768, 3072], P(None, ('dp', 'seq')), may hold values from -0.21875 to 0.21875
- down_weight: float32 [2, 3072, 768], P(None, ('dp', 'seq')), may hold values from -0.109375 to 0.109375
- down_moment: float32 [2, 3072, 768], P(None, ('dp', 'seq')), may hold values from -256 to 256
- down_average: float32 [2, 3072, 768], P(None, ('dp', 'seq')), may hold values from -0.109375 to 0.109375
- layer_vectors: float32 [2, 8, 768], P(None, None, ('dp', 'seq')), may hold values from -0.6 to 1.6
- vector_moment: float32 [2, 8, 768], P(None, None, ('dp', 'seq')), may hold values from -256 to 256
- vector_average: float32 [2, 8, 768], P(None, None, ('dp', 'seq')), may hold values from -0.6 to 1.6
- hidden_bias: float32 [2, 3072], P(None, ('dp', 'seq')), may hold values from -1.5 to 1.5
- bias_moment: float32 [2, 3072], P(None, ('dp', 'seq')), may hold values from -112 to 112
- bias_average: float32 [2, 3072], P(None, ('dp', 'seq')), may hold values from -1.5 to 1.5
Outputs:
- output: bfloat16 [8, 1024, 768], P('dp', 'seq')
- input_grad: bfloat16 [8, 1024, 768], P('dp', 'seq')
- attention_grad: float32 [2, 4, 768, 768], P(None, None, ('dp', 'seq'))
- attention_moment_new: float32 [2, 4, 768, 768], P(None, None, ('dp', 'seq'))
- attention_average_new: float32 [2, 4, 768, 768], P(None, None, ('dp', 'seq'))
- attention_weight_new: float32 [2, 4, 768, 768], P(None, None, ('dp', 'seq'))
- attention_weight_copy: bfloat16 [2, 4, 768, 768], P(None, None, ('dp', 'seq'))
- up_grad: float32 [2, 768, 3072], P(None, ('dp', 'seq'))
- up_moment_new: float32 [2, 768, 3072], P(None, ('dp', 'seq'))
- up_average_new: float32 [2, 768, 3072], P(None, ('dp', 'seq'))
- up_weight_new: float32 [2, 768, 3072], P(None, ('dp', 'seq'))
- up_weight_copy: bfloat16 [2, 768, 3072], P(None, ('dp', 'seq'))
- down_grad: float32 [2, 3072, 768], P(None, ('dp', 'seq'))
- down_moment_new: float32 [2, 3072, 768], P(None, ('dp', 'seq'))
- down_average_new: float32 [2, 3072, 768], P(None, ('dp', 'seq'))
- down_weight_new: float32 [2, 3072, 768], P(None, ('dp', 'seq'))
- down_weight_copy: bfloat16 [2, 3072, 768], P(None, ('dp', 'seq'))
- vector_grad: float32 [2, 8, 768], P(None, None, ('dp', 'seq'))
- vector_moment_new: float32 [2, 8, 768], P(None, None, ('dp', 'seq'))
- vector_average_new: float32 [2, 8, 768], P(None, None, ('dp', 'seq'))
- layer_vectors_new: float32 [2, 8, 768], P(None, None, ('dp', 'seq'))
- layer_vectors_copy: bfloat16 [2, 8, 768], P(None, None, ('dp', 'seq'))
- bias_grad: float32 [2, 3072], P(None, ('dp', 'seq'))
- bias_moment_new: float32 [2, 3072], P(None, ('dp', 'seq'))
- bias_average_new: float32 [2, 3072], P(None, ('dp', 'seq'))
- hidden_bias_new: float32 [2, 3072], P(None, ('dp', 'seq'))
- hidden_bias_copy: bfloat16 [2, 3072], P(None, ('dp', 'seq'))
Inputs may be any that keep to these rules, and one draw needn't show every extreme that they name: `image_lengths`: in each row the first 7 entries are image lengths and the last is the padding; a row's entries sum to 1024, and its largest entry is 384.
All inputs are finite; a program needn't handle non-finite values.
Results may differ from a plain program's by a relative error of at most 0.014.
Values may be sent and summed in bfloat16 or wider, within the bound.
A program may use at most 320 MiB of HBM per device.

v0:
```python
import math

import jax
import jax.numpy as jnp
from jax import lax
from jax.sharding import PartitionSpec as P

HEAD_DIM = 64
SEGS = 8


EPSILON = 1e-06
SCALE_SCORE = 0.125
MOMENTUM_RATE = 0.9
DECAY_RATE = 0.0001
AVERAGE_RATE = 0.5
LEARN_BASE = 0.1


def as_sent(shard):
    return jax.tree.map(lambda a: a.astype(jnp.bfloat16) if a.dtype == jnp.float32 else a, shard)


def layer_norm(values, gain_row, shift_row):
    center = values - jnp.mean(values, axis=-1, keepdims=True)
    spread = jnp.mean(center * center, axis=-1, keepdims=True)
    return center * lax.rsqrt(spread + EPSILON) * gain_row + shift_row


def gelu_exact(values):
    return jax.nn.gelu(values, approximate=False)


def project(values, matrix):
    return jnp.einsum("rti,ij->rtj", values, matrix, preferred_element_type=jnp.float32)


def project_back(grad_rows, matrix):
    return jnp.einsum("rtj,ij->rti", grad_rows, matrix, preferred_element_type=jnp.float32)


def outer_sum(values, grad_rows):
    return jnp.einsum("rti,rtj->ij", values, grad_rows, preferred_element_type=jnp.float32)


def column_sum(grad_rows):
    return jnp.sum(grad_rows, axis=(0, 1), dtype=jnp.float32)


def segment_ids(image_lengths, row_len):
    bounds = jnp.cumsum(image_lengths, axis=-1, dtype=jnp.int32)
    places = jnp.arange(row_len, dtype=jnp.int32)
    return jnp.sum(
        (bounds[:, None, :] <= places[None, :, None]).astype(jnp.int32), axis=-1, dtype=jnp.int32
    )


def visible_block(seg_rows, offset, block_size):
    row_len = seg_rows.shape[0]
    seg_query = seg_rows[offset : offset + block_size]
    matching = seg_query[:, None] == seg_rows[None, :]
    open_key = seg_rows[None, :] != SEGS - 1
    query_place = offset + jnp.arange(block_size, dtype=jnp.int32)
    key_place = jnp.arange(row_len, dtype=jnp.int32)
    return matching & open_key | (query_place[:, None] == key_place[None, :])


def score_block(query_block, key_heads, seg_rows, offset):
    scores = (
        jnp.einsum("qhd,khd->hqk", query_block, key_heads, preferred_element_type=jnp.float32)
        * SCALE_SCORE
    )
    allowed = visible_block(seg_rows, offset, query_block.shape[0])
    return jnp.where(allowed[None], scores, -1e30)


def split_heads(row_values):
    return row_values.reshape(row_values.shape[0], row_values.shape[1] // HEAD_DIM, HEAD_DIM)


def attend_row(row_items):
    query_row, key_row, value_row, seg_rows = row_items
    row_len = query_row.shape[0]
    query_heads = split_heads(query_row)
    key_heads = split_heads(key_row)
    value_heads = split_heads(value_row)
    block_size = min(512, row_len)
    outputs = []
    totals = []
    for offset in range(0, row_len, block_size):
        scores = score_block(query_heads[offset : offset + block_size], key_heads, seg_rows, offset)
        top_score = jnp.max(scores, axis=-1, keepdims=True)
        exponent = jnp.exp(scores - top_score)
        denominator = jnp.sum(exponent, axis=-1, keepdims=True)
        probability = (exponent / denominator).astype(jnp.bfloat16)
        outputs.append(
            jnp.einsum("hqk,khd->qhd", probability, value_heads, preferred_element_type=jnp.float32)
        )
        totals.append(top_score[..., 0] + jnp.log(denominator[..., 0]))
    mixture = jnp.concatenate(outputs, axis=0).reshape(query_row.shape).astype(jnp.bfloat16)
    return (mixture, jnp.concatenate(totals, axis=1))


def attend_back(row_items):
    query_row, key_row, value_row, grad_row, log_total, seg_rows = row_items
    row_len = query_row.shape[0]
    query_heads = split_heads(query_row)
    key_heads = split_heads(key_row)
    value_heads = split_heads(value_row)
    grad_heads = split_heads(grad_row)
    block_size = min(512, row_len)
    key_grad = jnp.zeros(key_heads.shape, jnp.float32)
    value_grad = jnp.zeros(value_heads.shape, jnp.float32)
    query_grads = []
    for offset in range(0, row_len, block_size):
        query_block = query_heads[offset : offset + block_size]
        grad_block = grad_heads[offset : offset + block_size]
        scores = score_block(query_block, key_heads, seg_rows, offset)
        probability = jnp.exp(scores - log_total[:, offset : offset + block_size, None])
        prob_low = probability.astype(jnp.bfloat16)
        prob_grad = jnp.einsum(
            "qhd,khd->hqk", grad_block, value_heads, preferred_element_type=jnp.float32
        )
        inner_sum = jnp.sum(probability * prob_grad, axis=-1, keepdims=True)
        score_grad = (probability * (prob_grad - inner_sum)).astype(jnp.bfloat16)
        query_grads.append(
            jnp.einsum("hqk,khd->qhd", score_grad, key_heads, preferred_element_type=jnp.float32)
            * SCALE_SCORE
        )
        key_grad = (
            key_grad
            + jnp.einsum(
                "hqk,qhd->khd", score_grad, query_block, preferred_element_type=jnp.float32
            )
            * SCALE_SCORE
        )
        value_grad = value_grad + jnp.einsum(
            "hqk,qhd->khd", prob_low, grad_block, preferred_element_type=jnp.float32
        )
    flat_shape = query_row.shape
    query_grad = jnp.concatenate(query_grads, axis=0)
    return (
        query_grad.reshape(flat_shape).astype(jnp.bfloat16),
        key_grad.reshape(flat_shape).astype(jnp.bfloat16),
        value_grad.reshape(flat_shape).astype(jnp.bfloat16),
    )


def layer_forward(hidden_in, params, seg_full):
    attention, upward, downward, vectors, bias_up = params
    vector_values = vectors.astype(jnp.float32)
    normed = layer_norm(hidden_in, vector_values[0], vector_values[1]).astype(jnp.bfloat16)
    queries = (project(normed, attention[0]) + vector_values[2]).astype(jnp.bfloat16)
    key_rows = project(normed, attention[1]).astype(jnp.bfloat16)
    value_rows = (project(normed, attention[2]) + vector_values[3]).astype(jnp.bfloat16)
    query_full, key_full, value_full = (
        lax.all_to_all(queries, "seq", split_axis=2, concat_axis=1, tiled=True),
        lax.all_to_all(key_rows, "seq", split_axis=2, concat_axis=1, tiled=True),
        lax.all_to_all(value_rows, "seq", split_axis=2, concat_axis=1, tiled=True),
    )
    mixture, log_total = lax.map(attend_row, (query_full, key_full, value_full, seg_full))
    mixed_tokens = lax.all_to_all(mixture, "seq", split_axis=1, concat_axis=2, tiled=True)
    residual = hidden_in + (project(mixed_tokens, attention[3]) + vector_values[4])
    normed_two = layer_norm(residual, vector_values[5], vector_values[6]).astype(jnp.bfloat16)
    hidden_pre = project(normed_two, upward) + bias_up.astype(jnp.float32)
    hidden_act = gelu_exact(hidden_pre).astype(jnp.bfloat16)
    result = residual + (project(hidden_act, downward) + vector_values[7])
    saved_values = (
        hidden_in,
        normed,
        query_full,
        key_full,
        value_full,
        log_total,
        mixed_tokens,
        residual,
        normed_two,
        hidden_pre,
        hidden_act,
    )
    return (result, saved_values)


def layer_backward(grad_out, params, saved_values, seg_full):
    attention, upward, downward, vectors, bias_up = params
    vector_values = vectors.astype(jnp.float32)
    (
        hidden_in,
        normed,
        query_full,
        key_full,
        value_full,
        log_total,
        mixed_tokens,
        residual,
        normed_two,
        hidden_pre,
        hidden_act,
    ) = saved_values
    grad_mlp = grad_out.astype(jnp.bfloat16)
    grad_down = outer_sum(hidden_act, grad_mlp)
    grad_act = project_back(grad_mlp, downward)
    grad_pre = jax.vjp(gelu_exact, hidden_pre)[1](grad_act)[0].astype(jnp.bfloat16)
    grad_up = outer_sum(normed_two, grad_pre)
    grad_normed_two = project_back(grad_pre, upward)
    norm_pull_two = jax.vjp(layer_norm, residual, vector_values[5], vector_values[6])[1]
    grad_resid_norm, grad_gain_two, grad_shift_two = norm_pull_two(grad_normed_two)
    grad_residual = grad_out + grad_resid_norm
    grad_proj = grad_residual.astype(jnp.bfloat16)
    grad_outproj = outer_sum(mixed_tokens, grad_proj)
    grad_mixed = project_back(grad_proj, attention[3]).astype(jnp.bfloat16)
    grad_heads = lax.all_to_all(grad_mixed, "seq", split_axis=2, concat_axis=1, tiled=True)
    query_grad, key_grad, value_grad = lax.map(
        attend_back, (query_full, key_full, value_full, grad_heads, log_total, seg_full)
    )
    grad_query, grad_key, grad_value = (
        lax.all_to_all(query_grad, "seq", split_axis=1, concat_axis=2, tiled=True),
        lax.all_to_all(key_grad, "seq", split_axis=1, concat_axis=2, tiled=True),
        lax.all_to_all(value_grad, "seq", split_axis=1, concat_axis=2, tiled=True),
    )
    grad_wq = outer_sum(normed, grad_query)
    grad_wk = outer_sum(normed, grad_key)
    grad_wv = outer_sum(normed, grad_value)
    grad_normed = (
        project_back(grad_query, attention[0])
        + project_back(grad_key, attention[1])
        + project_back(grad_value, attention[2])
    )
    norm_pull_one = jax.vjp(layer_norm, hidden_in, vector_values[0], vector_values[1])[1]
    grad_in_norm, grad_gain_one, grad_shift_one = norm_pull_one(grad_normed)
    grad_in = grad_residual + grad_in_norm
    attention_terms = jnp.stack([grad_wq, grad_wk, grad_wv, grad_outproj])
    vector_terms = jnp.stack(
        [
            grad_gain_one,
            grad_shift_one,
            column_sum(grad_query),
            column_sum(grad_value),
            column_sum(grad_proj),
            grad_gain_two,
            grad_shift_two,
            column_sum(grad_mlp),
        ]
    )
    return (grad_in, (attention_terms, grad_up, grad_down, vector_terms, column_sum(grad_pre)))


def fold_terms(terms, dims, dp_count, seq_count):
    folded = []
    for member in range(len(terms)):
        term = terms[member]
        place = dims[member]
        shape = term.shape
        leading = math.prod(shape[:place])
        owned = shape[place] // (dp_count * seq_count)
        trailing = owned * math.prod(shape[place + 1 :])
        folded.append(term.reshape(leading, dp_count, seq_count, trailing))
    return tuple(folded)


def unfold_terms(received, terms, dims, dp_count, seq_count):
    results = []
    for member in range(len(terms)):
        shape = terms[member].shape
        place = dims[member]
        owned_shape = shape[:place] + (shape[place] // (dp_count * seq_count),) + shape[place + 1 :]
        results.append(jnp.sum(received[member], axis=(1, 2)).reshape(owned_shape))
    return tuple(results)


def optimizer_step(gradient, master, moment, average, step_rate):
    direction = gradient + DECAY_RATE * master
    moment_new = MOMENTUM_RATE * moment + direction
    master_new = master - step_rate * (direction + MOMENTUM_RATE * moment_new)
    average_new = AVERAGE_RATE * average + (1.0 - AVERAGE_RATE) * master_new
    return (gradient, moment_new, average_new, master_new, master_new.astype(jnp.bfloat16))


def per_device(
    inputs,
    cotangent,
    image_lengths,
    attention_weight,
    attention_moment,
    attention_average,
    up_weight,
    up_moment,
    up_average,
    down_weight,
    down_moment,
    down_average,
    layer_vectors,
    vector_moment,
    vector_average,
    hidden_bias,
    bias_moment,
    bias_average,
):
    masters = (attention_weight, up_weight, down_weight, layer_vectors, hidden_bias)
    layer_count = attention_weight.shape[0]
    dp_count = lax.axis_size("dp")
    seq_count = lax.axis_size("seq")
    seg_full = segment_ids(image_lengths, inputs.shape[1] * seq_count)

    def gather_layer(level_index):
        pieces = tuple((master[level_index].astype(jnp.bfloat16) for master in masters))
        return (
            lax.all_gather(pieces[0], ("dp", "seq"), axis=1, tiled=True),
            lax.all_gather(pieces[1], ("dp", "seq"), axis=0, tiled=True),
            lax.all_gather(pieces[2], ("dp", "seq"), axis=0, tiled=True),
            lax.all_gather(pieces[3], ("dp", "seq"), axis=1, tiled=True),
            lax.all_gather(pieces[4], ("dp", "seq"), axis=0, tiled=True),
        )

    hidden = inputs.astype(jnp.float32)
    kept_params = []
    kept_saved = []
    for level_index in range(layer_count):
        params = gather_layer(level_index)
        hidden, saved_values = layer_forward(hidden, params, seg_full)
        kept_params.append(params)
        kept_saved.append(saved_values)
    output = hidden.astype(jnp.bfloat16)
    stack_dims = (2, 1, 1, 2, 1)
    grad_hidden = cotangent.astype(jnp.float32)
    layer_terms = [None] * layer_count
    for level_index in reversed(range(layer_count)):
        params = kept_params[level_index]
        grad_hidden, terms_here = layer_backward(
            grad_hidden, params, kept_saved[level_index], seg_full
        )
        layer_terms[level_index] = terms_here
    stacked = tuple(
        (jnp.stack([terms_here[member] for terms_here in layer_terms]) for member in range(5))
    )
    folded = fold_terms(stacked, stack_dims, dp_count, seq_count)
    received = jax.tree.map(
        lambda part, own: part.astype(own.dtype),
        lax.all_to_all(
            lax.all_to_all(as_sent(folded), "dp", split_axis=1, concat_axis=1, tiled=True),
            "seq",
            split_axis=2,
            concat_axis=2,
            tiled=True,
        ),
        folded,
    )
    reduced = unfold_terms(received, stacked, stack_dims, dp_count, seq_count)
    total_tokens = inputs.shape[0] * inputs.shape[1] * dp_count * seq_count
    step_rate = LEARN_BASE / math.sqrt(total_tokens)
    states = (
        (attention_weight, attention_moment, attention_average),
        (up_weight, up_moment, up_average),
        (down_weight, down_moment, down_average),
        (layer_vectors, vector_moment, vector_average),
        (hidden_bias, bias_moment, bias_average),
    )
    outcome = [output, grad_hidden.astype(jnp.bfloat16)]
    for member in range(5):
        master, moment, average = states[member]
        outcome.extend(optimizer_step(reduced[member], master, moment, average, step_rate))
    return tuple(outcome)


def solution(mesh):
    placed = (
        P("dp", "seq", None),
        P("dp", "seq", None),
        P("dp", None),
        P(None, None, ("dp", "seq"), None),
        P(None, None, ("dp", "seq"), None),
        P(None, None, ("dp", "seq"), None),
        P(None, ("dp", "seq"), None),
        P(None, ("dp", "seq"), None),
        P(None, ("dp", "seq"), None),
        P(None, ("dp", "seq"), None),
        P(None, ("dp", "seq"), None),
        P(None, ("dp", "seq"), None),
        P(None, None, ("dp", "seq")),
        P(None, None, ("dp", "seq")),
        P(None, None, ("dp", "seq")),
        P(None, ("dp", "seq")),
        P(None, ("dp", "seq")),
        P(None, ("dp", "seq")),
    )
    return jax.shard_map(
        per_device,
        mesh=mesh,
        in_specs=placed,
        out_specs=(
            P("dp", "seq", None),
            P("dp", "seq", None),
            P(None, None, ("dp", "seq"), None),
            P(None, None, ("dp", "seq"), None),
            P(None, None, ("dp", "seq"), None),
            P(None, None, ("dp", "seq"), None),
            P(None, None, ("dp", "seq"), None),
            P(None, ("dp", "seq"), None),
            P(None, ("dp", "seq"), None),
            P(None, ("dp", "seq"), None),
            P(None, ("dp", "seq"), None),
            P(None, ("dp", "seq"), None),
            P(None, ("dp", "seq"), None),
            P(None, ("dp", "seq"), None),
            P(None, ("dp", "seq"), None),
            P(None, ("dp", "seq"), None),
            P(None, ("dp", "seq"), None),
            P(None, None, ("dp", "seq")),
            P(None, None, ("dp", "seq")),
            P(None, None, ("dp", "seq")),
            P(None, None, ("dp", "seq")),
            P(None, None, ("dp", "seq")),
            P(None, ("dp", "seq")),
            P(None, ("dp", "seq")),
            P(None, ("dp", "seq")),
            P(None, ("dp", "seq")),
            P(None, ("dp", "seq")),
        ),
        check_vma=False,
    )
```

profile of v0, /device:TPU:0, one launch (start us, length us, event | category | flops | bytes accessed | tf_op | source)
XLA Modules:
  0.0 1679.4 jit_solution(9455039014948862140)
XLA Ops:
  13.8 44.7 %all-gather = bf16[1,8,768]{1,0,2:T(2,128)(2,1)S(1)} all-gather(bf16[1,8,24]{1,0,2:T(2,128)(2,1)S(1)} %get-tuple-element.204), channel_id=2, replica_groups=mesh['dp'=8,'seq'=4] {'dp','seq'}, dimensions={2}, use_global_device_ids=true | all-gather | bytes 12672 | tf_op jit(solution)/shard_map/all_gather | solution.py:311
  58.9 19.9 %slice_reduce_fusion.8 = (f32[768]{0:T(1024)}, f32[768]{0:T(1024)S(1)}, f32[768]{0:T(1024)S(1)}, f32[768]{0:T(1024)}, f32[768]{0:T(1024)S(1)}, /*index=5*/f32[768]{0:T(1024)S(1)}, f32[768]{0:T(1024)S(1)}, f32[768]{0:T(1024)S(1)}) fusion(f32[1,8,768]{1,0,2:T(1,128)S(1)} %convert_element_type.505), kind=kLoop, calls=%fused_computation.271 | loop fusion | bytes 49152 | tf_op jit(solution)/shard_map/slice | solution.py:167
  114.2 40.4 %all-reduce.2 = (bf16[3072]{0:T(1024)(128)(2,1)S(1)}, bf16[3072]{0:T(1024)(128)(2,1)}) all-reduce(bf16[3072]{0:T(1024)(128)(2,1)S(1)} %dynamic-update-slice, bf16[3072]{0:T(1024)(128)(2,1)S(1)} %dynamic-update-slice.1), channel_id=5, replica_groups=mesh['dp'=8,'seq'=4] {'dp','seq'}, use_global_device_ids=true, to_apply=%add | all-reduce | flops 6144 | bytes 24576
  155.3 42.0 %all-gather.5 = bf16[1,8,768]{1,0,2:T(2,128)(2,1)S(1)} all-gather(bf16[1,8,24]{1,0,2:T(2,128)(2,1)S(1)} %get-tuple-element.203), channel_id=7, replica_groups=mesh['dp'=8,'seq'=4] {'dp','seq'}, dimensions={2}, use_global_device_ids=true | all-gather | bytes 12672 | tf_op jit(solution)/shard_map/all_gather | solution.py:311
  219.5 4.9 reduce.92
  229.2 20.0 %slice_reduce_fusion = (f32[768]{0:T(1024)}, f32[768]{0:T(1024)S(1)}, f32[768]{0:T(1024)S(1)}, f32[768]{0:T(1024)S(1)}, f32[768]{0:T(1024)S(1)}, /*index=5*/f32[768]{0:T(1024)S(1)}, f32[768]{0:T(1024)S(1)}, f32[768]{0:T(1024)S(1)}) fusion(f32[1,8,768]{1,0,2:T(1,128)S(1)} %convert_element_type.507), kind=kLoop, calls=%fused_computation.263 | loop fusion | bytes 49152 | tf_op jit(solution)/shard_map/slice | solution.py:167
  256.2 12.2 multiply_convert_fusion.5
  351.3 8.4 all-to-all-done.7
  365.9 11.7 multiply_convert_fusion.4
  377.6 31.2 %all-gather.27.cloned.1.call-done = bf16[1,3072,768]{2,1,0:T(8,128)(2,1)} async-done(((bf16[1,96,768]{2,1,0:T(8,128)(2,1)}), bf16[1,3072,768]{2,1,0:T(8,128)(2,1)}) %all-gather.27.cloned.1.call-update) | async-done | bytes 4718608 | tf_op jit(solution)/shard_map/all_gather | solution.py:310
  408.8 7.0 fusion.221
  430.1 7.3 all-to-all-done.8
  464.9 5.7 reduce.98
  547.0 4.4 all-to-all-done.12
  575.5 5.7 reduce.102
  647.2 6.0 all-to-all-start.22
  653.3 5.2 convolution_convert_fusion.2
  658.4 8.3 stack.177
  672.0 5.2 convolution_convert_fusion.3
  677.2 8.2 stack.176
  690.5 9.1 pad_maximum_fusion.1
  700.2 6.2 all-to-all-start.18
  706.5 5.0 convolution_convert_fusion
  711.5 8.4 stack.180
  719.8 5.0 convolution_convert_fusion.1
  724.8 8.3 stack.179
  733.1 9.1 pad_maximum_fusion.2
  742.2 170.5 %all-to-all-done.18 = bf16[2,8,4,73728]{3,2,0,1:T(4,128)(2,1)} async-done(((bf16[2,8,4,73728]{3,2,0,1:T(4,128)(2,1)}), bf16[2,8,4,73728]{3,2,0,1:T(4,128)(2,1)}, u32[]{:S(2)}, u32[]{:S(2)}) %all-to-all-start.18) | async-done | bytes 9437216 | tf_op jit(solution)/shard_map/all_to_all | solution.py:340
  912.7 5.1 all-to-all-start.20
  929.0 8.3 pad_maximum_fusion
  937.3 15.3 convert_element_type.484
  952.6 9.2 copy.265
  961.8 161.3 %all-to-all-done.20 = bf16[2,8,4,73728]{3,2,0,1:T(4,128)(2,1)} async-done(((bf16[2,8,4,73728]{3,2,0,1:T(4,128)(2,1)}), bf16[2,8,4,73728]{3,2,0,1:T(4,128)(2,1)}, u32[]{:S(2)}, u32[]{:S(2)}) %all-to-all-start.20) | async-done | bytes 9437216 | tf_op jit(solution)/shard_map/all_to_all | solution.py:340
  1123.1 5.5 all-to-all-start.16
  1128.6 12.4 copy.269
  1141.1 192.1 %all-to-all-done.16 = bf16[8,8,4,18432]{3,2,0,1:T(4,128)(2,1)} async-done(((bf16[8,8,4,18432]{3,2,0,1:T(4,128)(2,1)}), bf16[8,8,4,18432]{3,2,0,1:T(4,128)(2,1)}, u32[]{:S(2)}, u32[]{:S(2)}) %all-to-all-start.16) | async-done | bytes 9437216 | tf_op jit(solution)/shard_map/all_to_all | solution.py:340
  1333.1 5.8 all-to-all-start.19
  1338.9 12.5 copy.272
  1351.4 91.9 %all-to-all-done.19 = bf16[2,8,4,73728]{3,1,0,2:T(8,128)(2,1)} async-done(((bf16[2,8,4,73728]{3,1,0,2:T(8,128)(2,1)}), bf16[2,8,4,73728]{3,1,0,2:T(8,128)(2,1)}, u32[]{:S(2)}, u32[]{:S(2)}) %all-to-all-start.19) | async-done | bytes 9437216 | tf_op jit(solution)/shard_map/all_to_all | solution.py:339
  1443.3 6.0 all-to-all-start.21
  1449.4 12.4 copy.266
  1461.8 92.0 %all-to-all-done.21 = bf16[2,8,4,73728]{3,1,0,2:T(8,128)(2,1)} async-done(((bf16[2,8,4,73728]{3,1,0,2:T(8,128)(2,1)}), bf16[2,8,4,73728]{3,1,0,2:T(8,128)(2,1)}, u32[]{:S(2)}, u32[]{:S(2)}) %all-to-all-start.21) | async-done | bytes 9437216 | tf_op jit(solution)/shard_map/all_to_all | solution.py:339
  1553.8 5.8 all-to-all-start.17
  1559.7 5.0 fusion.102
  1569.3 6.3 convert_reduce_fusion
  1577.9 6.3 convert_reduce_fusion.1
  1586.7 77.3 %all-to-all-done.17 = bf16[8,8,4,18432]{3,1,0,2:T(8,128)(2,1)} async-done(((bf16[8,8,4,18432]{3,1,0,2:T(8,128)(2,1)}), bf16[8,8,4,18432]{3,1,0,2:T(8,128)(2,1)}, u32[]{:S(2)}, u32[]{:S(2)}) %all-to-all-start.17) | async-done | bytes 9437216 | tf_op jit(solution)/shard_map/all_to_all | solution.py:339
  1664.0 6.0 convert_reduce_fusion.2
  (757 shorter events, 404.9 us)
Async XLA Ops:
  7.2 72.7 %all-gather.17.cloned.1.call-start = ((), (), s32[]{:S(2)}) async-start(), calls=%async_computation.26 | async-start | bytes 4866048 | tf_op jit(solution)/shard_map/all_gather | solution.py:308
  9.2 246.9 %all-gather.19.cloned.1.call-start = ((), (), s32[]{:S(2)}) async-start(), calls=%async_computation.27 | async-start | bytes 4866048 | tf_op jit(solution)/shard_map/all_gather | solution.py:309
  11.1 67.8 %copy-start.8 = (bf16[1,256,768]{2,1,0:T(8,128)(2,1)S(1)}, bf16[1,256,768]{2,1,0:T(8,128)(2,1)}, u32[]{:S(2)}) copy-start(bf16[1,256,768]{2,1,0:T(8,128)(2,1)} %param.18) | copy-start | bytes 1179652
  11.1 257.3 %all-gather.21.cloned.1.call-start = ((), (), s32[]{:S(2)}) async-start(), calls=%async_computation.28 | async-start | bytes 4866048 | tf_op jit(solution)/shard_map/all_gather | solution.py:310
  11.2 68.1 %copy-start.184 = (s32[1,8]{1,0:T(1,128)S(1)}, s32[1,8]{1,0:T(1,128)}, u32[]{:S(2)}) copy-start(s32[1,8]{1,0:T(1,128)} %param.20) | copy-start | bytes 100
  12.0 264.6 %all-gather.23.cloned.1.call-start = ((), (), s32[]{:S(2)}) async-start(), calls=%async_computation.29 | async-start | bytes 4866048 | tf_op jit(solution)/shard_map/all_gather | solution.py:308
  12.5 353.3 %all-gather.25.cloned.1.call-start = ((), (), s32[]{:S(2)}) async-start(), calls=%async_computation.30 | async-start | bytes 4866048 | tf_op jit(solution)/shard_map/all_gather | solution.py:309
  13.1 395.7 %all-gather.27.cloned.1.call-start = ((), (), s32[]{:S(2)}) async-start(), calls=%async_computation.31 | async-start | bytes 4866048 | tf_op jit(solution)/shard_map/all_gather | solution.py:310
  78.8 177.3 %copy-start.100 = (f32[768]{0:T(1024)}, f32[768]{0:T(1024)S(1)}, u32[]{:S(2)}) copy-start(f32[768]{0:T(1024)S(1)} %get-tuple-element.146) | copy-start | bytes 9220
  86.8 11.1 all-to-all-start
  97.9 11.7 all-to-all-start.1
  109.6 45.7 %copy-start.72 = (bf16[4,2,24576]{2,1,0:T(2,128)(2,1)}, bf16[4,2,24576]{2,1,0:T(2,128)(2,1)S(1)}, u32[]{:S(2)}) copy-start(bf16[4,2,24576]{2,1,0:T(2,128)(2,1)S(1)} %all-to-all-done.1) | copy-start | bytes 1179652
  109.6 92.8 %all-to-all-start.2 = ((bf16[4,2,24576]{2,1,0:T(2,128)(2,1)}), bf16[4,2,24576]{2,1,0:T(2,128)(2,1)}, u32[]{:S(2)}, u32[]{:S(2)}) async-start(bf16[4,2,24576]{2,1,0:T(2,128)(2,1)} %reshape.1225), calls=%async_computation.2 | async-start | bytes 786432 | tf_op jit(solution)/shard_map/all_to_all | solution.py:158
  225.7 23.5 %all-to-all-start.3 = ((bf16[4,2,24576]{2,1,0:T(2,128)(2,1)}), bf16[4,2,24576]{2,1,0:T(2,128)(2,1)S(1)}, u32[]{:S(2)}, u32[]{:S(2)}) async-start(bf16[4,2,24576]{2,1,0:T(2,128)(2,1)} %reshape.1227), calls=%async_computation.3 | async-start | bytes 786432 | tf_op jit(solution)/shard_map/all_to_all | solution.py:162
  272.8 90.8 %copy-start.10 = (f32[1,256,768]{2,1,0:T(8,128)}, f32[1,256,768]{2,1,0:T(8,128)S(1)}, u32[]{:S(2)}) copy-start(f32[1,256,768]{2,1,0:T(8,128)S(1)} %get-tuple-element.219) | copy-start | bytes 2359300
  273.3 27.7 %copy-start.27 = (bf16[256,768]{1,0:T(8,128)(2,1)}, bf16[256,768]{1,0:T(8,128)(2,1)S(1)}, u32[]{:S(2)}) copy-start(bf16[256,768]{1,0:T(8,128)(2,1)S(1)} %fusion.162) | copy-start | bytes 1179652
  284.9 11.8 all-to-all-start.4
  296.7 14.6 all-to-all-start.5
  311.3 11.6 all-to-all-start.6
  347.8 11.9 all-to-all-start.7
  365.6 52.3 %copy-start.12 = (f32[1,256,768]{2,1,0:T(8,128)}, f32[1,256,768]{2,1,0:T(8,128)S(1)}, u32[]{:S(2)}) copy-start(f32[1,256,768]{2,1,0:T(8,128)S(1)} %get-tuple-element.225) | copy-start | bytes 2359300
  365.6 52.3 %copy-start.134 = (f32[256]{0:T(256)}, f32[256]{0:T(256)S(1)}, u32[]{:S(2)}) copy-start(f32[256]{0:T(256)S(1)} %broadcast_multiply_fusion) | copy-start | bytes 3076
  365.8 52.1 %copy-start.140 = (f32[256]{0:T(256)}, f32[256]{0:T(256)S(1)}, u32[]{:S(2)}) copy-start(f32[256]{0:T(256)S(1)} %fusion.177) | copy-start | bytes 3076
  365.9 42.9 %copy-start.31 = (bf16[1,256,768]{2,1,0:T(8,128)(2,1)S(1)}, bf16[1,256,768]{2,1,0:T(8,128)(2,1)}, u32[]{:S(2)}) copy-start(bf16[1,256,768]{2,1,0:T(8,128)(2,1)} %param.19) | copy-start | bytes 1179652
  426.4 11.0 all-to-all-start.8
  430.1 25.7 %copy-start.98 = (f32[3,512]{1,0:T(4,128)}, f32[3,512]{1,0:T(4,128)S(1)}, u32[]{:S(2)}) copy-start(f32[3,512]{1,0:T(4,128)S(1)} %log_add_fusion.2) | copy-start | bytes 18436
  473.0 18.8 %all-to-all-start.9 = ((bf16[4,2,24576]{2,1,0:T(2,128)(2,1)}), bf16[4,2,24576]{2,1,0:T(2,128)(2,1)}, u32[]{:S(2)}, u32[]{:S(2)}) async-start(bf16[4,2,24576]{2,1,0:T(2,128)(2,1)} %reshape.1239), calls=%async_computation.9 | async-start | bytes 786432 | tf_op jit(solution)/shard_map/all_to_all | solution.py:217
  491.8 13.7 all-to-all-start.10
  505.5 11.3 all-to-all-start.11
  509.4 56.6 %copy-start.96 = (f32[3,512]{1,0:T(4,128)}, f32[3,512]{1,0:T(4,128)S(1)}, u32[]{:S(2)}) copy-start(f32[3,512]{1,0:T(4,128)S(1)} %log_add_fusion) | copy-start | bytes 18436
  540.4 11.0 all-to-all-start.12
  583.6 18.7 %all-to-all-start.13 = ((bf16[4,2,24576]{2,1,0:T(2,128)(2,1)}), bf16[4,2,24576]{2,1,0:T(2,128)(2,1)}, u32[]{:S(2)}, u32[]{:S(2)}) async-start(bf16[4,2,24576]{2,1,0:T(2,128)(2,1)} %reshape.1247), calls=%async_computation.13 | async-start | bytes 786432 | tf_op jit(solution)/shard_map/all_to_all | solution.py:217
  602.3 14.5 all-to-all-start.14
  616.8 15.5 all-to-all-start.15
  632.3 15.0 all-to-all-start.24
  647.2 20.9 %all-to-all-start.22 = ((bf16[8,2,768]{2,1,0:T(2,128)(2,1)}), bf16[8,2,768]{2,1,0:T(2,128)(2,1)}, u32[]{:S(2)}, u32[]{:S(2)}) async-start(bf16[8,2,768]{2,1,0:T(2,128)(2,1)} %reshape.1253), calls=%async_computation.22 | async-start | bytes 49152 | tf_op jit(solution)/shard_map/all_to_all | solution.py:340
  668.1 19.1 %all-to-all-start.25 = ((bf16[2,8,4,96]{3,1,0,2:T(8,128)(2,1)}), bf16[2,8,4,96]{3,1,0,2:T(8,128)(2,1)}, u32[]{:S(2)}, u32[]{:S(2)}) async-start(bf16[2,8,4,96]{3,1,0,2:T(8,128)(2,1)} %copy.279), calls=%async_computation.25 | async-start | bytes 32768 | tf_op jit(solution)/shard_map/all_to_all | solution.py:339
  687.2 12.4 all-to-all-start.23
  700.2 212.4 %all-to-all-start.18 = ((bf16[2,8,4,73728]{3,2,0,1:T(4,128)(2,1)}), bf16[2,8,4,73728]{3,2,0,1:T(4,128)(2,1)}, u32[]{:S(2)}, u32[]{:S(2)}) async-start(bf16[2,8,4,73728]{3,2,0,1:T(4,128)(2,1)} %pad_maximum_fusion.1), calls=%async_computation.18 | async-start | bytes 18874368 | tf_op jit(solution)/shard_map/all_to_all | solution.py:340
  912.7 210.4 %all-to-all-start.20 = ((bf16[2,8,4,73728]{3,2,0,1:T(4,128)(2,1)}), bf16[2,8,4,73728]{3,2,0,1:T(4,128)(2,1)}, u32[]{:S(2)}, u32[]{:S(2)}) async-start(bf16[2,8,4,73728]{3,2,0,1:T(4,128)(2,1)} %pad_maximum_fusion.2), calls=%async_computation.20 | async-start | bytes 18874368 | tf_op jit(solution)/shard_map/all_to_all | solution.py:340
  1123.1 210.0 %all-to-all-start.16 = ((bf16[8,8,4,18432]{3,2,0,1:T(4,128)(2,1)}), bf16[8,8,4,18432]{3,2,0,1:T(4,128)(2,1)}, u32[]{:S(2)}, u32[]{:S(2)}) async-start(bf16[8,8,4,18432]{3,2,0,1:T(4,128)(2,1)} %copy.265), calls=%async_computation.16 | async-start | bytes 18874368 | tf_op jit(solution)/shard_map/all_to_all | solution.py:340
  1333.1 110.2 %all-to-all-start.19 = ((bf16[2,8,4,73728]{3,1,0,2:T(8,128)(2,1)}), bf16[2,8,4,73728]{3,1,0,2:T(8,128)(2,1)}, u32[]{:S(2)}, u32[]{:S(2)}) async-start(bf16[2,8,4,73728]{3,1,0,2:T(8,128)(2,1)} %copy.269), calls=%async_computation.19 | async-start | bytes 18874368 | tf_op jit(solution)/shard_map/all_to_all | solution.py:339
  1443.3 110.4 %all-to-all-start.21 = ((bf16[2,8,4,73728]{3,1,0,2:T(8,128)(2,1)}), bf16[2,8,4,73728]{3,1,0,2:T(8,128)(2,1)}, u32[]{:S(2)}, u32[]{:S(2)}) async-start(bf16[2,8,4,73728]{3,1,0,2:T(8,128)(2,1)} %copy.272), calls=%async_computation.21 | async-start | bytes 18874368 | tf_op jit(solution)/shard_map/all_to_all | solution.py:339
  1461.8 97.8 %copy-start.171 = (f32[768]{0:T(1024)S(1)}, f32[768]{0:T(1024)}, u32[]{:S(2)}) copy-start(f32[768]{0:T(1024)} %get-tuple-element.137) | copy-start | bytes 9220
  1553.8 110.2 %all-to-all-start.17 = ((bf16[8,8,4,18432]{3,1,0,2:T(8,128)(2,1)}), bf16[8,8,4,18432]{3,1,0,2:T(8,128)(2,1)}, u32[]{:S(2)}, u32[]{:S(2)}) async-start(bf16[8,8,4,18432]{3,1,0,2:T(8,128)(2,1)} %copy.266), calls=%async_computation.17 | async-start | bytes 18874368 | tf_op jit(solution)/shard_map/all_to_all | solution.py:339
  1585.7 84.3 %copy-start.53 = (f32[2,24,3072]{2,1,0:T(8,128)}, f32[2,24,3072]{2,1,0:T(8,128)S(1)}, u32[]{:S(2)}) copy-start(f32[2,24,3072]{2,1,0:T(8,128)S(1)} %get-tuple-element.172) | copy-start | bytes 1769476
  1586.7 83.5 %copy-start.50 = (f32[2,4,24,768]{3,2,1,0:T(8,128)S(1)}, f32[2,4,24,768]{3,2,1,0:T(8,128)}, u32[]{:S(2)}) copy-start(f32[2,4,24,768]{3,2,1,0:T(8,128)} %param.21) | copy-start | bytes 1769476
  1586.7 83.5 %copy-start.85 = (f32[2,4,24,768]{3,2,1,0:T(8,128)S(1)}, f32[2,4,24,768]{3,2,1,0:T(8,128)}, u32[]{:S(2)}) copy-start(f32[2,4,24,768]{3,2,1,0:T(8,128)} %param.22) | copy-start | bytes 1769476
  (183 other events, 1218.2 us)
Sparse Core Ops, SparseCore 0:
  11.5 66.7 all-gather.16
  81.8 63.1 all-gather.18
  148.5 62.1 all-gather.20
  214.0 62.5 all-gather.22
  279.9 63.1 all-gather.24
  346.4 62.3 all-gather.26
where the time goes:
time: 1690 us; the launch traced here: 1680 us
  waiting for transfers between devices  846 us (50%)
  local copies, waits for them, and re-layouts  260 us (15%)
  matrix products  164 us (10%)
  other arithmetic  151 us (9%)
  blocking collectives  127 us (8%)
  starting transfers between devices  113 us (7%)
  between operations  18 us (1%)
    all_to_all x5, waiting for transfers between devices, per_device(): lax.all_to_all(as_sent(folded), 'dp', split_axis=1, concat_axis=1, tiled=...  524 us
    all_to_all x5, waiting for transfers between devices, per_device(): lax.all_to_all(lax.all_to_all(as_sent(folded), 'dp', split_axis=1, concat...  261 us
    all_gather x2, blocking collectives, gather_layer(): lax.all_gather(pieces[3], ('dp', 'seq'), axis=1, tiled=True)  86.7 us
    unnamed x450, local copies, waits for them, and re-layouts  63.6 us
    unnamed x22, other arithmetic  63.2 us
    dot_general x12, matrix products, project(): jnp.einsum('rti,ij->rtj', values, matrix, preferred_element_type=jnp.floa...  48.6 us
    unnamed x1, blocking collectives  40.4 us
    slice x2, local copies, waits for them, and re-layouts, layer_forward(): result = residual + (project(hidden_act, downward) + vector_values[7])  39.9 us
  transfers between devices with their start and end apart: 32, of which 15 were waited for; matrix products, arithmetic and copies ran while one was open for 27% of the time, Pallas kernels for 0%

commit v1 on v0

--- a/solution.py
+++ b/solution.py
@@ -1,8 +1,11 @@
+import functools
 import math
 
 import jax
 import jax.numpy as jnp
 from jax import lax
+from jax.experimental import pallas as pl
+from jax.experimental.pallas import tpu as pltpu
 from jax.sharding import PartitionSpec as P
 
 HEAD_DIM = 64
@@ -15,6 +18,7 @@
 DECAY_RATE = 0.0001
 AVERAGE_RATE = 0.5
 LEARN_BASE = 0.1
+VMEM_BYTES = 66500000
 
 
 def as_sent(shard):
@@ -48,7 +52,8 @@
 
 
 def segment_ids(image_lengths, row_len):
-    bounds = jnp.cumsum(image_lengths, axis=-1, dtype=jnp.int32)
+    upto = jnp.arange(SEGS)[:, None] <= jnp.arange(SEGS)[None, :]
+    bounds = jnp.sum(jnp.where(upto[None], image_lengths[:, :, None], 0), axis=1, dtype=jnp.int32)
     places = jnp.arange(row_len, dtype=jnp.int32)
     return jnp.sum(
         (bounds[:, None, :] <= places[None, :, None]).astype(jnp.int32), axis=-1, dtype=jnp.int32
@@ -276,6 +281,890 @@
     return (gradient, moment_new, average_new, master_new, master_new.astype(jnp.bfloat16))
 
 
+def plain_step(inputs, cotangent, image_lengths, masters):
+    layer_count = masters[0].shape[0]
+    dp_count = lax.axis_size("dp")
+    seq_count = lax.axis_size("seq")
+    seg_full = segment_ids(image_lengths, inputs.shape[1] * seq_count)
+
+    def gather_layer(level_index):
+        pieces = tuple((master[level_index].astype(jnp.bfloat16) for master in masters))
+        return (
+            lax.all_gather(pieces[0], ("dp", "seq"), axis=1, tiled=True),
+            lax.all_gather(pieces[1], ("dp", "seq"), axis=0, tiled=True),
+            lax.all_gather(pieces[2], ("dp", "seq"), axis=0, tiled=True),
+            lax.all_gather(pieces[3], ("dp", "seq"), axis=1, tiled=True),
+            lax.all_gather(pieces[4], ("dp", "seq"), axis=0, tiled=True),
+        )
+
+    hidden = inputs.astype(jnp.float32)
+    kept_params = []
+    kept_saved = []
+    for level_index in range(layer_count):
+        params = gather_layer(level_index)
+        hidden, saved_values = layer_forward(hidden, params, seg_full)
+        kept_params.append(params)
+        kept_saved.append(saved_values)
+    output = hidden.astype(jnp.bfloat16)
+    stack_dims = (2, 1, 1, 2, 1)
+    grad_hidden = cotangent.astype(jnp.float32)
+    layer_terms = [None] * layer_count
+    for level_index in reversed(range(layer_count)):
+        params = kept_params[level_index]
+        grad_hidden, terms_here = layer_backward(
+            grad_hidden, params, kept_saved[level_index], seg_full
+        )
+        layer_terms[level_index] = terms_here
+    stacked = tuple(
+        (jnp.stack([terms_here[member] for terms_here in layer_terms]) for member in range(5))
+    )
+    folded = fold_terms(stacked, stack_dims, dp_count, seq_count)
+    received = jax.tree.map(
+        lambda part, own: part.astype(own.dtype),
+        lax.all_to_all(
+            lax.all_to_all(as_sent(folded), "dp", split_axis=1, concat_axis=1, tiled=True),
+            "seq",
+            split_axis=2,
+            concat_axis=2,
+            tiled=True,
+        ),
+        folded,
+    )
+    reduced = unfold_terms(received, stacked, stack_dims, dp_count, seq_count)
+    return (output, grad_hidden.astype(jnp.bfloat16), *reduced)
+
+
+MESH = pl.DeviceIdType.MESH
+F32 = jnp.float32
+BF16 = jnp.bfloat16
+KEYS = 896
+QBLOCK = 256
+
+
+def nt(left, right):
+    return lax.dot_general(left, right, (((1,), (1,)), ((), ())), preferred_element_type=F32)
+
+
+def nn(left, right):
+    return lax.dot_general(left, right, (((1,), (0,)), ((), ())), preferred_element_type=F32)
+
+
+def tn(left, right):
+    return lax.dot_general(left, right, (((0,), (0,)), ((), ())), preferred_element_type=F32)
+
+
+def norm_parts(values):
+    center = values - jnp.mean(values, axis=-1, keepdims=True)
+    scale = lax.rsqrt(jnp.mean(center * center, axis=-1, keepdims=True) + EPSILON)
+    return center * scale, scale
+
+
+def norm_back(values, grad, gain):
+    unit, scale = norm_parts(values)
+    pulled = grad * gain
+    first = jnp.mean(pulled, axis=-1, keepdims=True)
+    second = jnp.mean(pulled * unit, axis=-1, keepdims=True)
+    result = scale * (pulled - first - unit * second)
+    return (
+        result,
+        jnp.sum(grad * unit, axis=0, keepdims=True),
+        jnp.sum(grad, axis=0, keepdims=True),
+    )
+
+
+SEMS = 400
+
+
+def step_kernel(NZ, x_in, cot_in, lens, aw, uw, dw, lv, hb, *rest):
+    (out, gin, gA, gU, gD, gV, gB) = rest[:7]
+    (
+        w1, w2, w3, w4, stg, rsl, gm, a, b, qh, kk, vv, kT, vT, oh, ofull, goh, gos, gpo, lse,
+        x1, xs, hact, gpb, segc, segr, facc, gq, gw1, gw2, gw3, gw4, gw5, xl1, xl2, xl3, xl4, xl5,
+        zl1, zl2, zl3, zl4, zl5, ps1, ps2, ps3, ps5, pl1, pl2, pl3, pl5, tt, V, vg, snd, rcv,
+        credx, credz,
+    ) = rest[7:]
+    W = {1: w1, 2: w2, 3: w3, 4: w4}
+    GW = {1: gw1, 2: gw2, 3: gw3, 4: gw4, 5: gw5}
+    XL = {1: xl1, 2: xl2, 3: xl3, 4: xl4, 5: xl5}
+    ZL = {1: zl1, 2: zl2, 3: zl3, 4: zl4, 5: zl5}
+    PS = {1: ps1, 2: ps2, 3: ps3, 5: ps5}
+    PL = {1: pl1, 2: pl2, 3: pl3, 5: pl5}
+    S = 4
+    T, D = x_in.shape[1], x_in.shape[2]
+    R = aw.shape[2]
+    CH = R * S
+    DP = NZ * 2
+    FJ = hb.shape[1]
+
+    d = lax.axis_index("dp")
+    s = lax.axis_index("seq")
+    z, x = d // 2, d % 2
+    y, c = s // 2, s % 2
+    xp = 1 - x
+
+    def xor(k):
+        return ((y + k // 2) % 2) * 2 + (c + k % 2) % 2
+
+    def dev(dd, ss):
+        return {"dp": dd, "seq": ss}
+
+    core_peer, y_peer, x_peer = dev(d, xor(1)), dev(d, xor(2)), dev(z * 2 + xp, s)
+
+    def zdev(dz):
+        return dev(((z + dz) % NZ) * 2 + x, s)
+
+    count = [0]
+
+    def sems(n):
+        first = count[0]
+        count[0] += n
+        assert count[0] <= SEMS
+        return first
+
+    def rc(src, dst, device, i):
+        return pltpu.make_async_remote_copy(
+            src_ref=src, dst_ref=dst, send_sem=snd.at[i], recv_sem=rcv.at[i],
+            device_id=device, device_id_type=MESH,
+        )
+
+    pending = []
+    sent_weights = []
+
+    def flush():
+        for copy in pending:
+            copy.wait_send()
+        pending.clear()
+
+    def rows(i):
+        return pl.ds(pl.multiple_of(i * T, T), T)
+
+    def chunk(i):
+        return pl.ds(pl.multiple_of(i * CH, CH), CH)
+
+    class Gather:
+        def __init__(self, view):
+            i = sems(3)
+            own, across = view.at[rows(s)], view.at[rows(xor(2))]
+            self.c1 = rc(own, own, core_peer, i)
+            self.c2 = rc(own, own, y_peer, i + 1)
+            self.c3 = rc(across, across, core_peer, i + 2)
+
+        def start(self):
+            self.c2.start()
+            self.c1.start()
+
+        def core(self):
+            self.c1.wait_recv()
+
+        def forward(self):
+            self.c2.wait_recv()
+            self.c3.start()
+
+        def last(self):
+            self.c3.wait_recv()
+
+        def done(self):
+            pending.extend([self.c1, self.c2, self.c3])
+
+    ag_sems = {}
+
+    def ag_start(g, l):
+        zi, xi = sems(NZ), sems(NZ)
+        ag_sems[g, l] = (zi, xi)
+        own = W[g].at[l, chunk(d)]
+        for dz in range(1, NZ):
+            rc(own, own, zdev(dz), zi + dz).start()
+            sent_weights.append((g, zi + dz))
+
+    def ag_forward(g, l):
+        zi, xi = ag_sems[g, l]
+        for dz in range(NZ):
+            part = W[g].at[l, chunk(((z - dz + NZ) % NZ) * 2 + x)]
+            if dz:
+                rc(part, part, zdev(dz), zi + dz).wait_recv()
+            rc(part, part, x_peer, xi + dz).start()
+            sent_weights.append((g, xi + dz))
+
+    def ag_done(g, l):
+        xi = ag_sems[g, l][1]
+        for dz in range(NZ):
+            part = W[g].at[l, chunk(dz)]
+            rc(part, part, x_peer, xi + dz).wait_recv()
+
+    red_sems = {}
+
+    def x_copies(g, l):
+        i = red_sems[g, l]
+        return [rc(GW[g].at[chunk(zi * 2 + xp)], XL[g].at[zi], x_peer, i + zi) for zi in range(NZ)]
+
+    def z_copies(g, l):
+        i = red_sems[g, l] + NZ
+        return [
+            rc(GW[g].at[chunk(((z + dz) % NZ) * 2 + x)], ZL[g].at[dz - 1], zdev(dz), i + dz)
+            for dz in range(1, NZ)
+        ]
+
+    def s_copies(g, l):
+        i = red_sems[g, l] + 2 * NZ
+        return [
+            rc(PS[g].at[(s + ds) % S], PL[g].at[s], dev(d, (s + ds) % S), i + ds)
+            for ds in range(1, S)
+        ]
+
+    def red_x(g, l):
+        if l == 0 and g != 5:
+            pl.semaphore_wait(credx.at[g], 1)
+        red_sems[g, l] = sems(2 * NZ + S)
+        for copy in x_copies(g, l):
+            copy.start()
+
+    def red_z(g, l):
+        for zi, copy in enumerate(x_copies(g, l)):
+            copy.wait_recv()
+            mine = chunk(zi * 2 + x)
+            GW[g][mine] = (GW[g][mine].astype(F32) + XL[g][zi].astype(F32)).astype(BF16)
+        if l == 1 and g != 5:
+            pl.semaphore_signal(credx.at[g], 1, device_id=x_peer, device_id_type=MESH)
+        if l == 0 and g != 5:
+            pl.semaphore_wait(credz.at[g], NZ - 1)
+        for copy in z_copies(g, l):
+            copy.start()
+
+    def red_sum(g, l):
+        total = GW[g][chunk(d)].astype(F32)
+        for k, copy in enumerate(z_copies(g, l)):
+            copy.wait_recv()
+            total = total + ZL[g][k].astype(F32)
+        for copy in x_copies(g, l) + z_copies(g, l):
+            copy.wait_send()
+        if l == 1 and g != 5:
+            for dz in range(1, NZ):
+                pl.semaphore_signal(credz.at[g], 1, device_id=zdev(dz), device_id_type=MESH)
+        if g == 4:
+            gD[l] = total
+            return
+        if g == 5:
+            tt[0:CH, :] = total
+        wide = total.shape[1]
+        for k in range(S):
+            piece = jnp.concatenate(
+                [total[R * k : R * (k + 1)], jnp.zeros((PS[g].shape[1] - R, wide), F32)], axis=0
+            )
+            PS[g][k] = piece.astype(BF16)
+        PL[g][s] = PS[g][s]
+        for copy in s_copies(g, l):
+            copy.start()
+
+    def red_write(g, l):
+        for copy in s_copies(g, l):
+            copy.wait_recv()
+        parts = [PL[g][k].astype(F32)[0:R] for k in range(S)]
+        if g == 1:
+            gA[l, 0] = jnp.concatenate([p[:, 0:192] for p in parts], axis=1)
+            gA[l, 1] = jnp.concatenate(
+                [q for p in parts for q in (p[:, 256:384], p[:, 192:256])], axis=1
+            )
+            gA[l, 2] = jnp.concatenate([p[:, 384:576] for p in parts], axis=1)
+        elif g == 2:
+            gA[l, 3] = parts[0] + parts[1] + parts[2] + parts[3]
+        elif g == 3:
+            gU[l] = jnp.concatenate(
+                [parts[k][:, FJ * i : FJ * (i + 1)] for i in range(DP) for k in range(S)], axis=1
+            )
+        else:
+            biases = jnp.transpose(tt[...])
+            tt[0:R, :] = parts[0] + parts[1] + parts[2] + parts[3]
+            vectors = jnp.transpose(tt[...])
+            for k in range(2):
+                gV[k] = vectors[16 * k : 16 * k + 8, 0:R]
+                gB[k : k + 1, :] = biases[16 * k + 8 : 16 * k + 9, 0:CH]
+        for copy in s_copies(g, l):
+            copy.wait_send()
+
+    parity = [0]
+
+    class Scatter:
+        def __init__(self):
+            i = sems(3)
+            base = parity[0] * 3
+            parity[0] = 1 - parity[0]
+            self.base = base
+            self.r0 = rc(stg.at[0:T], rsl.at[base], core_peer, i)
+            self.r1 = rc(stg.at[T : 2 * T], rsl.at[base + 1], core_peer, i + 1)
+            self.r2 = rc(stg.at[2 * T : 3 * T], rsl.at[base + 2], y_peer, i + 2)
+
+        def send_core(self, j):
+            k = 0 if j == 3 else 1
+            stg[T * k : T * (k + 1)] = facc[T * j : T * (j + 1)].astype(BF16)
+            (self.r0 if j == 3 else self.r1).start()
+
+        def send_y(self):
+            self.r0.wait_recv()
+            stg[2 * T : 3 * T] = (
+                facc[2 * T : 3 * T] + rsl[self.base].astype(F32)
+            ).astype(BF16)
+            self.r2.start()
+
+        def finish(self):
+            self.r1.wait_recv()
+            self.r2.wait_recv()
+            total = facc[0:T] + rsl[self.base + 1].astype(F32) + rsl[self.base + 2].astype(F32)
+            for copy in (self.r0, self.r1, self.r2):
+                copy.wait_send()
+            return total
+
+    barrier = pltpu.get_barrier_semaphore()
+    greeted = [core_peer, y_peer, dev(d, xor(3)), x_peer] + [zdev(dz) for dz in range(1, NZ)]
+    for device in greeted:
+        pl.semaphore_signal(barrier, inc=1, device_id=device, device_id_type=MESH)
+
+    tt[...] = jnp.zeros_like(tt)
+    tt[64:72, 0:R] = lv[0]
+    tt[72:80, 0:R] = lv[1]
+    tt[80:82, 0:CH] = hb[...]
+    turned = jnp.transpose(tt[...])
+    lane128 = lax.broadcasted_iota(jnp.int32, (1, 128), 1)
+    vec_cols = jnp.where(lane128 < 80, turned[0:R, :], 0.0)[:, 64:128]
+    bias_cols = jnp.where((lane128 >= 80) & (lane128 < 82), turned[0:CH, :], 0.0)
+    for k in range(S):
+        o = 192 * k
+        two = []
+        for l in range(2):
+            wq, wk, wv = aw[l, 0], aw[l, 1], aw[l, 2]
+            tail = vec_cols if l == 0 else jnp.zeros((R, 64), F32)
+            two.append(
+                jnp.concatenate(
+                    [wq[:, o : o + 192], wk[:, o + 128 : o + 192], wk[:, o : o + 128],
+                     wv[:, o : o + 192], tail],
+                    axis=1,
+                )
+            )
+        stg[144 * k : 144 * k + 48, 0:640] = jnp.concatenate(two, axis=0).astype(BF16)
+    gm[0, rows(s)] = x_in[0]
+
+    pl.semaphore_wait(barrier, len(greeted))
+
+    def piece_rows(k):
+        return pl.multiple_of(k * 144, 16)
+
+    i = sems(S)
+    pieces1 = []
+    for ds in (2, 3, 1):
+        to = xor(ds)
+        copy = rc(stg.at[pl.ds(piece_rows(to), 48), 0:640], rsl.at[s, 0:48, 0:640], dev(d, to), i + ds)
+        copy.start()
+        pieces1.append(copy)
+    gather_x = Gather(gm.at[0])
+    gather_x.start()
+    for k in range(S):
+        two = [
+            jnp.concatenate(
+                [uw[l][:, (m * S + k) * FJ : (m * S + k + 1) * FJ] for m in range(DP)], axis=1
+            )
+            for l in range(2)
+        ]
+        stg[144 * k + 48 : 144 * k + 96, :] = jnp.concatenate([aw[0, 3], aw[1, 3]], axis=0).astype(BF16)
+        stg[144 * k + 96 : 144 * k + 144, :] = jnp.concatenate(two, axis=0).astype(BF16)
+    i = sems(S)
+    pieces2 = []
+    for ds in (2, 3, 1):
+        to = xor(ds)
+        copy = rc(
+            stg.at[pl.ds(pl.multiple_of(piece_rows(to) + 48, 16), 96), :],
+            rsl.at[s, 48:144, :], dev(d, to), i + ds,
+        )
+        copy.start()
+        pieces2.append(copy)
+    rsl[s, 0:48, 0:640] = stg[pl.ds(piece_rows(s), 48), 0:640]
+    rsl[s, 48:144, :] = stg[pl.ds(pl.multiple_of(piece_rows(s) + 48, 16), 96), :]
+    vg[...] = jnp.zeros_like(vg)
+    for l in range(2):
+        w4[l, chunk(d)] = dw[l].astype(BF16)
+    for copy in pieces1:
+        copy.wait_recv()
+    got = [rsl[k, 0:48, 0:640].astype(F32) for k in range(S)]
+    for l in range(2):
+        full = jnp.concatenate([g[R * l : R * (l + 1)] for g in got], axis=0)
+        if l == 0:
+            full = jnp.concatenate([full[:, 0:512], full[:, 512:640] + bias_cols], axis=1)
+        w1[l, chunk(d)] = full.astype(BF16)
+    ag_start(1, 0)
+
+    bounds = []
+    running = jnp.int32(0)
+    for k in range(SEGS):
+        running = running + lens[0, k]
+        bounds.append(running)
+    N = S * T
+
+    def segments(shape, dim):
+        place = lax.broadcasted_iota(jnp.int32, shape, dim)
+        seg = jnp.zeros(shape, jnp.int32)
+        for bound in bounds:
+            seg = seg + jnp.where(place >= bound, 1, 0)
+        return jnp.where(seg == SEGS - 1, SEGS + place, seg)
+
+    segr[...] = segments((8, N), 1)
+    segc[...] = segments((N, 128), 0)
+
+    for copy in pieces2:
+        copy.wait_recv()
+    for g, at in ((2, 48), (3, 96)):
+        got = [rsl[k, at : at + 48, :].astype(F32) for k in range(S)]
+        for l in range(2):
+            W[g][l, chunk(d)] = jnp.concatenate(
+                [part[R * l : R * (l + 1)] for part in got], axis=0
+            ).astype(BF16)
+    for copy in pieces1 + pieces2:
+        copy.wait_send()
+    ag_start(2, 0)
+    ag_forward(1, 0)
+    ag_start(3, 0)
+    gather_x.core()
+    gather_x.forward()
+    gm[1, rows(s)] = cot_in[0]
+    ag_done(1, 0)
+    V[...] = jnp.transpose(w1[0, :, 512:640].astype(F32))[64:96]
+    gather_x.last()
+    gather_x.done()
+
+    def vec(l, k):
+        return V[8 * l + k : 8 * l + k + 1, :]
+
+    def own_heads(row):
+        total = jnp.zeros((1, 192), F32)
+        for k in range(S):
+            total = total + jnp.where(s == k, row[:, 192 * k : 192 * (k + 1)], 0.0)
+        return total
+
+    def at_heads(part):
+        total = jnp.zeros((1, D), F32)
+        for k in range(S):
+            spread = [jnp.zeros((1, 192), F32)] * S
+            spread[k] = part
+            total = total + jnp.where(s == k, jnp.concatenate(spread, axis=1), 0.0)
+        return total
+
+    low = lax.broadcasted_iota(jnp.int32, (T, 128), 1) < 64
+    low_rows = lax.broadcasted_iota(jnp.int32, (128, QBLOCK), 0) < 64
+
+    def project_heads(l):
+        bias = jnp.concatenate(
+            [own_heads(vec(l, 2)), jnp.zeros((1, 192), F32), own_heads(vec(l, 3)), jnp.zeros((1, 64), F32)],
+            axis=1,
+        )
+
+        @pl.loop(0, S)
+        def _(i):
+            r = rows(i)
+            if l == 0:
+                unit, _ = norm_parts(gm[0, r].astype(F32))
+                a[0, r] = (unit * vec(0, 0) + vec(0, 1)).astype(BF16)
+            full = (nn(a[l, r], w1[l]) + bias).astype(BF16).astype(F32)
+            t0, t1, t2, t3, t4 = (full[:, 128 * j : 128 * (j + 1)] for j in range(5))
+            t1r = pltpu.roll(t1, 64, 1)
+            v4 = jnp.where(low, t4, 0.0)
+            qh[l, 0, r] = (jnp.where(low, t0, 0.0) * SCALE_SCORE).astype(BF16)
+            qh[l, 1, r] = (jnp.where(low, 0.0, t0) * SCALE_SCORE).astype(BF16)
+            qh[l, 2, r] = (jnp.where(low, t1, 0.0) * SCALE_SCORE).astype(BF16)
+            kk[l, 0, r] = t2.astype(BF16)
+            kk[l, 1, r] = t1r.astype(BF16)
+            vv[l, 0, r] = t3.astype(BF16)
+            vv[l, 1, r] = v4.astype(BF16)
+            kT[l, 0, :, r] = jnp.transpose(t2).astype(BF16)
+            kT[l, 1, :, r] = jnp.transpose(t1r).astype(BF16)
+            vT[0, :, r] = jnp.transpose(t3).astype(BF16)
+            vT[1, :, r] = jnp.transpose(v4).astype(BF16)
+
+    def query_block(qb):
+        q = pl.ds(pl.multiple_of(qb * QBLOCK, QBLOCK), QBLOCK)
+        k = pl.ds(pl.multiple_of((qb // 2) * (N - KEYS), 128), KEYS)
+        return q, k
+
+    def attend(l, points):
+        @pl.loop(0, N // QBLOCK)
+        def _(qb):
+            for at, action in points.items():
+                pl.when(qb == at)(action)
+            q, k = query_block(qb)
+            allowed = jnp.concatenate([segc[k, :]] * 2, axis=1) == segr[0:1, q]
+            parts = []
+            for h in range(3):
+                scores = jnp.where(allowed, nt(kk[l, h // 2, k], qh[l, h, q]), -1e30)
+                top = jnp.max(scores, axis=0, keepdims=True)
+                grown = jnp.exp(scores - top)
+                total = jnp.sum(grown, axis=0, keepdims=True)
+                lse[l, h : h + 1, q] = top + jnp.log(total)
+                parts.append(nn(vT[h // 2, :, k], grown.astype(BF16)) / total)
+            oh[l, q, 0:128] = jnp.transpose(jnp.where(low_rows, parts[0], parts[1])).astype(BF16)
+            oh[l, q, 128:256] = jnp.transpose(parts[2]).astype(BF16)
+
+    def attend_grad(l, points):
+        facc[:, 0:512] = jnp.zeros((N, 512), F32)
+
+        @pl.loop(0, N // QBLOCK)
+        def _(qb):
+            for at, action in points.items():
+                pl.when(qb == at)(action)
+            q, k = query_block(qb)
+            allowed = jnp.concatenate([segc[k, :]] * 2, axis=1) == segr[0:1, q]
+            tiles = [goh[q, 0:128], goh[q, 128:256]]
+            inner = [
+                jnp.transpose(tiles[j].astype(F32) * oh[l, q, 128 * j : 128 * (j + 1)].astype(F32))
+                for j in range(2)
+            ]
+            inner = [
+                jnp.sum(inner[0][0:64], axis=0, keepdims=True),
+                jnp.sum(inner[0][64:128], axis=0, keepdims=True),
+                jnp.sum(inner[1], axis=0, keepdims=True),
+            ]
+            t0 = tiles[0].astype(F32)
+            heads = [
+                jnp.where(low, t0, 0.0).astype(BF16),
+                jnp.where(low, 0.0, t0).astype(BF16),
+                tiles[1],
+            ]
+            parts = []
+            for h in range(3):
+                p = h // 2
+                queries = qh[l, h, q]
+                scores = jnp.where(allowed, nt(kk[l, p, k], queries), -1e30)
+                prob = jnp.exp(scores - lse[l, h : h + 1, q])
+                grad = nt(vv[l, p, k], heads[h])
+                grad = (prob * (grad - inner[h])).astype(BF16)
+                facc[k, 256 + 128 * p : 384 + 128 * p] += nn(prob.astype(BF16), heads[h])
+                facc[k, 128 * p : 128 * (p + 1)] += nn(grad, queries)
+                parts.append(nn(kT[l, p, :, k], grad) * SCALE_SCORE)
+            gq[q, 0:128] = jnp.transpose(jnp.where(low_rows, parts[0], parts[1])).astype(BF16)
+            gq[q, 128:256] = jnp.transpose(jnp.where(low_rows, parts[2], 0.0)).astype(BF16)
+
+        @pl.loop(0, S)
+        def _(i):
+            r = rows(i)
+            other = pltpu.roll(facc[r, 128:256], 64, 1)
+            gq[r, 128:256] = (gq[r, 128:256].astype(F32) + other).astype(BF16)
+            gq[r, 256:384] = facc[r, 0:128].astype(BF16)
+            gq[r, 384:512] = facc[r, 256:384].astype(BF16)
+            gq[r, 512:640] = facc[r, 384:512].astype(BF16)
+
+    def exchange(source, target):
+        i = sems(S)
+        copies = []
+        for ds in (2, 3, 1):
+            to = xor(ds)
+            part = source(to)
+            copies.append(rc(part, target(s), dev(d, to), i + ds))
+        for copy in copies:
+            copy.start()
+        return copies
+
+    def mlp_forward(l, gather):
+        scatter = Scatter()
+
+        @pl.loop(0, S)
+        def _(k):
+            pl.when(k == 1)(gather.core)
+            pl.when(k == 2)(gather.forward)
+            pl.when(k == 3)(gather.last)
+            r = rows(((y + k // 2) % 2) * 2 + (c + k % 2) % 2)
+            pre = nn(b[l, r], w3[l]) + V[16 + l : 17 + l, :]
+            cdf = 0.5 * (1.0 + lax.erf(pre * 0.7071067811865476))
+            density = jnp.exp(-0.5 * pre * pre) * 0.3989422804014327
+            act = (pre * cdf).astype(BF16)
+            hact[l, r] = act
+            gpb[l, r] = (cdf + pre * density).astype(BF16)
+            facc[rows(k)] = nn(act, w4[l])
+            pl.when(k == 1)(lambda: scatter.send_core(1))
+            pl.when(k == 3)(lambda: scatter.send_core(3))
+
+        gather.done()
+        scatter.send_y()
+        return scatter
+
+    def mlp_backward(l, gather):
+        scatter = Scatter()
+        @pl.loop(0, S, init_carry=jnp.zeros((1, D), F32))
+        def bias_grad(i, carry):
+            if gather is None:
+                k = S - 1 - i
+            else:
+                k = i
+                pl.when(k == 1)(gather.core)
+                pl.when(k == 2)(gather.forward)
+                pl.when(k == 3)(gather.last)
+            r = rows(((y + k // 2) % 2) * 2 + (c + k % 2) % 2)
+            grad_act = nt(gm[l, r], w4[l])
+            grad_pre = (grad_act * gpb[l, r].astype(F32)).astype(BF16)
+            gpb[l, r] = grad_pre
+            facc[rows(k)] = nt(grad_pre, w3[l])
+            pl.when(k == 1)(lambda: scatter.send_core(1))
+            pl.when(k == 3)(lambda: scatter.send_core(3))
+            if gather is None:
+                pl.when(k == 2)(scatter.send_y)
+            return carry + jnp.sum(grad_pre.astype(F32), axis=0, keepdims=True)
+
+        vg[16 * l + 8 : 16 * l + 9, :] = bias_grad
+        if gather is not None:
+            gather.done()
+            scatter.send_y()
+        return scatter
+
+    def weight_grad(g, left, right):
+        @pl.loop(0, 2)
+        def _(i):
+            m = pl.ds(pl.multiple_of(i * 384, 384), 384)
+            GW[g][m, :] = tn(left(m), right()).astype(BF16)
+
+    def heads_input_grad(l):
+        scatter = Scatter()
+
+        @pl.loop(0, S)
+        def _(i):
+            k = S - 1 - i
+            r = rows(((y + k // 2) % 2) * 2 + (c + k % 2) % 2)
+            facc[rows(k)] = nt(gq[r], w1[l])
+            pl.when(k == 1)(lambda: scatter.send_core(1))
+            pl.when(k == 3)(lambda: scatter.send_core(3))
+            pl.when(k == 2)(scatter.send_y)
+
+        return scatter
+
+    def column(values):
+        return jnp.sum(values.astype(F32), axis=0, keepdims=True)
+
+    gather_cot = Gather(gm.at[1])
+    gather_b = {}
+    later = [
+        lambda: (ag_forward(2, 0), ag_start(4, 0)),
+        lambda: (ag_forward(3, 0), ag_start(1, 1)),
+        lambda: (ag_forward(4, 0), ag_start(2, 1)),
+        lambda: (ag_forward(1, 1), ag_start(3, 1)),
+        lambda: (ag_forward(2, 1), ag_start(4, 1)),
+        lambda: ag_forward(3, 1),
+        lambda: ag_forward(4, 1),
+    ]
+
+    def do_later():
+        later.pop(0)()
+
+    for l in range(2):
+        project_heads(l)
+        if l == 0:
+            gather_cot.start()
+        do_later()
+        if l == 0:
+            def point():
+                do_later()
+                gather_cot.core()
+                gather_cot.forward()
+            attend(l, {2: point})
+            gather_cot.last()
+            gather_cot.done()
+        else:
+            attend(l, {2: do_later})
+        copies = exchange(lambda to: oh.at[l, rows(to)], lambda me: goh.at[rows(me)])
+        goh[rows(s)] = oh[l, rows(s)]
+        pending.extend(copies)
+        ag_done(2, l)
+        for copy in copies:
+            copy.wait_recv()
+        ofull[l] = jnp.concatenate([goh[T * k : T * (k + 1)].astype(F32)[:, 0:192] for k in range(S)], axis=1).astype(BF16)
+        before = x_in[0].astype(F32) if l == 0 else xs[...]
+        middle = before + (nn(ofull[l], w2[l]) + vec(l, 4))
+        x1[l] = middle
+        unit, _ = norm_parts(middle)
+        b[l, rows(s)] = (unit * vec(l, 5) + vec(l, 6)).astype(BF16)
+        gather_b[l] = Gather(b.at[l])
+        gather_b[l].start()
+        if l == 0:
+            do_later()
+        ag_done(3, l)
+        ag_done(4, l)
+        scatter = mlp_forward(l, gather_b[l])
+        if l == 0:
+            do_later()
+        after = x1[l] + (scatter.finish() + vec(l, 7))
+        flush()
+        if l == 0:
+            xs[...] = after
+            unit, _ = norm_parts(after)
+            a[1, rows(s)] = (unit * vec(1, 0) + vec(1, 1)).astype(BF16)
+            gather_a = Gather(a.at[1])
+            gather_a.start()
+            do_later()
+            ag_done(1, 1)
+            gather_a.core()
+            gather_a.forward()
+            gather_a.last()
+            gather_a.done()
+            do_later()
+            later.insert(0, lambda: None)
+        else:
+            out[0] = after.astype(BF16)
+
+    grad = cot_in[0].astype(F32)
+    gather = None
+    for l in (1, 0):
+        first = l == 1
+        scatter = mlp_backward(l, gather)
+        if not first:
+            red_write(2, 1)
+            red_write(3, 1)
+            red_sum(1, 1)
+        vg[16 * l + 7 : 16 * l + 8, :] = column(gm[l, rows(s)])
+        weight_grad(4, lambda m: hact[l, :, m], lambda: gm[l])
+        red_x(4, l)
+        weight_grad(3, lambda m: b[l, :, m], lambda: gpb[l])
+        red_x(3, l)
+        grad_b = scatter.finish()
+        grad_x1, gain, shift = norm_back(x1[l], grad_b, vec(l, 5))
+        if first:
+            grad_x1 = grad_x1 + cot_in[0].astype(F32)
+        else:
+            grad_x1 = grad_x1 + xs[...]
+        x1[l] = grad_x1
+        vg[16 * l + 5 : 16 * l + 6, :] = gain
+        vg[16 * l + 6 : 16 * l + 7, :] = shift
+        gpo[...] = grad_x1.astype(BF16)
+        vg[16 * l + 4 : 16 * l + 5, :] = column(gpo[...])
+        flush()
+        back = nt(gpo[...], w2[l])
+        for k in range(S):
+            gos[k] = jnp.concatenate(
+                [back[:, 192 * k : 192 * (k + 1)], jnp.zeros((T, 64), F32)], axis=1
+            ).astype(BF16)
+        copies = exchange(lambda to: gos.at[to], lambda me: goh.at[rows(me)])
+        goh[rows(s)] = gos[s]
+        pending.extend(copies)
+        if not first:
+            red_write(1, 1)
+        weight_grad(2, lambda m: ofull[l, :, m], lambda: gpo[...])
+        red_x(2, l)
+        red_z(4, l)
+        for copy in copies:
+            copy.wait_recv()
+
+        def point_a():
+            red_z(3, l)
+
+        def point_b():
+            red_z(2, l)
+
+        attend_grad(l, {2: point_a, 3: point_b})
+        sums = column(gq[...])
+        vg[16 * l + 2 : 16 * l + 3, :] = at_heads(sums[:, 0:192])
+        vg[16 * l + 3 : 16 * l + 4, :] = at_heads(sums[:, 384:576])
+        scatter = heads_input_grad(l)
+        weight_grad(1, lambda m: a[l, :, m], lambda: gq[...])
+        red_x(1, l)
+        red_sum(4, l)
+        grad_a = scatter.finish()
+        before = xs[...] if first else x_in[0].astype(F32)
+        grad, gain, shift = norm_back(before, grad_a, vec(l, 0))
+        grad = grad + x1[l]
+        vg[16 * l : 16 * l + 1, :] = gain
+        vg[16 * l + 1 : 16 * l + 2, :] = shift
+        flush()
+        if first:
+            xs[...] = grad
+            gm[0, rows(s)] = grad.astype(BF16)
+            gather = Gather(gm.at[0])
+            gather.start()
+            red_sum(3, 1)
+            red_sum(2, 1)
+            red_z(1, 1)
+        else:
+            gin[0] = grad.astype(BF16)
+
+    gw5[...] = jnp.transpose(vg[...]).astype(BF16)
+    red_x(5, 0)
+    red_sum(3, 0)
+    red_sum(2, 0)
+    red_z(1, 0)
+    red_z(5, 0)
+    red_write(3, 0)
+    red_write(2, 0)
+    red_sum(1, 0)
+    red_sum(5, 0)
+    red_write(1, 0)
+    red_write(5, 0)
+    flush()
+    for g, i in sent_weights:
+        part = W[g].at[0, 0:CH]
+        rc(part, part, x_peer, i).wait_send()
+
+
+def fused_step(inputs, cotangent, image_lengths, attention, upward, downward, vectors, bias_up):
+    DP = lax.axis_size("dp")
+    S = lax.axis_size("seq")
+    NZ = DP // 2
+    L = attention.shape[0]
+    T, D = inputs.shape[1], inputs.shape[2]
+    N = S * T
+    R = attention.shape[2]
+    CH = R * S
+    RP = (R + 15) // 16 * 16
+    FJ = bias_up.shape[1]
+    vmem = pl.BlockSpec(memory_space=pltpu.VMEM)
+    V = pltpu.VMEM
+    widths = {1: 640, 2: D, 3: D, 4: D, 5: 128}
+    scratch = [
+        V((L, D, 640), BF16), V((L, D, D), BF16), V((L, D, D), BF16), V((L, D, D), BF16),
+        V((3 * T, D), BF16),
+        V((6, T, D), BF16),
+        V((L, N, D), BF16), V((L, N, D), BF16), V((L, N, D), BF16),
+        V((L, 3, N, 128), BF16), V((L, 2, N, 128), BF16), V((L, 2, N, 128), BF16),
+        V((L, 2, 128, N), BF16), V((2, 128, N), BF16),
+        V((L, N, 256), BF16), V((L, T, D), BF16),
+        V((N, 256), BF16), V((S, T, 256), BF16), V((T, D), BF16),
+        V((L, 8, N), F32),
+        V((L, T, D), F32), V((T, D), F32),
+        V((L, N, D), BF16), V((L, N, D), BF16),
+        V((N, 128), jnp.int32), V((8, N), jnp.int32),
+        V((N, D), F32),
+        V((N, 640), BF16),
+        *[V((D, widths[g]), BF16) for g in range(1, 6)],
+        *[V((NZ, CH, widths[g]), BF16) for g in range(1, 6)],
+        *[V((NZ - 1, CH, widths[g]), BF16) for g in range(1, 6)],
+        *[V((S, RP, widths[g]), BF16) for g in (1, 2, 3, 5)],
+        *[V((S, RP, widths[g]), BF16) for g in (1, 2, 3, 5)],
+        V((128, 128), F32), V((32, D), F32), V((128, D), F32),
+        pltpu.SemaphoreType.DMA((SEMS,)), pltpu.SemaphoreType.DMA((SEMS,)),
+        pltpu.SemaphoreType.REGULAR((8,)), pltpu.SemaphoreType.REGULAR((8,)),
+    ]
+    return pl.pallas_call(
+        functools.partial(step_kernel, NZ),
+        out_shape=(
+            jax.ShapeDtypeStruct(inputs.shape, BF16),
+            jax.ShapeDtypeStruct(inputs.shape, BF16),
+            jax.ShapeDtypeStruct(attention.shape, F32),
+            jax.ShapeDtypeStruct(upward.shape, F32),
+            jax.ShapeDtypeStruct(downward.shape, F32),
+            jax.ShapeDtypeStruct(vectors.shape, F32),
+            jax.ShapeDtypeStruct(bias_up.shape, F32),
+        ),
+        in_specs=[vmem, vmem, pl.BlockSpec(memory_space=pltpu.SMEM)] + [vmem] * 5,
+        out_specs=(vmem,) * 7,
+        scratch_shapes=scratch,
+        compiler_params=pltpu.CompilerParams(
+            collective_id=0, has_side_effects=True, vmem_limit_bytes=VMEM_BYTES
+        ),
+    )(inputs, cotangent, image_lengths, attention, upward, downward, vectors, bias_up)
+
+
+def fits_fused(inputs, attention, upward, bias_up, dp_count, seq_count):
+    own_rows, width = attention.shape[2], attention.shape[3]
+    return (
+        seq_count == 4
+        and dp_count == 8
+        and inputs.shape == (1, QBLOCK, 768)
+        and width == 768
+        and own_rows % 8 == 0
+        and upward.shape[2] == seq_count * width
+        and bias_up.shape[1] % 16 == 0
+    )
+
+
 def per_device(
     inputs,
     cotangent,
@@ -297,55 +1186,12 @@
     bias_average,
 ):
     masters = (attention_weight, up_weight, down_weight, layer_vectors, hidden_bias)
-    layer_count = attention_weight.shape[0]
     dp_count = lax.axis_size("dp")
     seq_count = lax.axis_size("seq")
-    seg_full = segment_ids(image_lengths, inputs.shape[1] * seq_count)
-
-    def gather_layer(level_index):
-        pieces = tuple((master[level_index].astype(jnp.bfloat16) for master in masters))
-        return (
-            lax.all_gather(pieces[0], ("dp", "seq"), axis=1, tiled=True),
-            lax.all_gather(pieces[1], ("dp", "seq"), axis=0, tiled=True),
-            lax.all_gather(pieces[2], ("dp", "seq"), axis=0, tiled=True),
-            lax.all_gather(pieces[3], ("dp", "seq"), axis=1, tiled=True),
-            lax.all_gather(pieces[4], ("dp", "seq"), axis=0, tiled=True),
-        )
-
-    hidden = inputs.astype(jnp.float32)
-    kept_params = []
-    kept_saved = []
-    for level_index in range(layer_count):
-        params = gather_layer(level_index)
-        hidden, saved_values = layer_forward(hidden, params, seg_full)
-        kept_params.append(params)
-        kept_saved.append(saved_values)
-    output = hidden.astype(jnp.bfloat16)
-    stack_dims = (2, 1, 1, 2, 1)
-    grad_hidden = cotangent.astype(jnp.float32)
-    layer_terms = [None] * layer_count
-    for level_index in reversed(range(layer_count)):
-        params = kept_params[level_index]
-        grad_hidden, terms_here = layer_backward(
-            grad_hidden, params, kept_saved[level_index], seg_full
-        )
-        layer_terms[level_index] = terms_here
-    stacked = tuple(
-        (jnp.stack([terms_here[member] for terms_here in layer_terms]) for member in range(5))
-    )
-    folded = fold_terms(stacked, stack_dims, dp_count, seq_count)
-    received = jax.tree.map(
-        lambda part, own: part.astype(own.dtype),
-        lax.all_to_all(
-            lax.all_to_all(as_sent(folded), "dp", split_axis=1, concat_axis=1, tiled=True),
-            "seq",
-            split_axis=2,
-            concat_axis=2,
-            tiled=True,
-        ),
-        folded,
-    )
-    reduced = unfold_terms(received, stacked, stack_dims, dp_count, seq_count)
+    if fits_fused(inputs, attention_weight, up_weight, hidden_bias, dp_count, seq_count):
+        output, input_grad, *reduced = fused_step(inputs, cotangent, image_lengths, *masters)
+    else:
+        output, input_grad, *reduced = plain_step(inputs, cotangent, image_lengths, masters)
     total_tokens = inputs.shape[0] * inputs.shape[1] * dp_count * seq_count
     step_rate = LEARN_BASE / math.sqrt(total_tokens)
     states = (
@@ -355,7 +1201,7 @@
         (layer_vectors, vector_moment, vector_average),
         (hidden_bias, bias_moment, bias_average),
     )
-    outcome = [output, grad_hidden.astype(jnp.bfloat16)]
+    outcome = [output, input_grad]
     for member in range(5):
         master, moment, average = states[member]
         outcome.extend(optimizer_step(reduced[member], master, moment, average, step_rate))

time: 1690 us -> 344 us (0.20)
  waiting for transfers between devices: 846 us -> 0 us
  Pallas kernels: 0 us -> 322 us
  local copies, waits for them, and re-layouts: 260 us -> 9.5 us
  matrix products: 164 us -> 0 us
  other arithmetic: 151 us -> 9.72 us
  blocking collectives: 127 us -> 0 us
  starting transfers between devices: 113 us -> 0 us
  between operations: 18 us -> 0.82 us
    all_to_all x26 -> x0, waiting for transfers between devices: 810 us -> none  [the longest x5 524 us: per_device(): lax.all_to_all(as_sent(folded), 'dp', split_axis=1, concat_axis=1, tiled=...]
    pallas_call x0 -> x1, Pallas kernels: none -> 322 us  [fused_step(): pl.pallas_call(functools.partial(step_kernel, NZ), out_shape=(jax.ShapeDt...]
    dot_general x60 -> x0, matrix products: 164 us -> none  [the longest x12 48.6 us: project(): jnp.einsum('rti,ij->rtj', values, matrix, preferred_element_type=jnp.floa...]
    all_to_all x26 -> x0, starting transfers between devices: 113 us -> none  [the longest x5 27.1 us: per_device(): lax.all_to_all(as_sent(folded), 'dp', split_axis=1, concat_axis=1, tiled=...]
    all_gather x2 -> x0, blocking collectives: 86.7 us -> none  [gather_layer(): lax.all_gather(pieces[3], ('dp', 'seq'), axis=1, tiled=True)]
    unnamed x22 -> x0, other arithmetic: 63.2 us -> none
    unnamed x450 -> x57, local copies, waits for them, and re-layouts: 63.6 us -> 9.5 us
    all_to_all x33 -> x0, local copies, waits for them, and re-layouts: 52.1 us -> none  [the longest x5 38.8 us: per_device(): lax.all_to_all(as_sent(folded), 'dp', split_axis=1, concat_axis=1, tiled=...]
  transfers between devices with their start and end apart: 32 -> 0, of which waited for: 15 -> 0; matrix products, arithmetic and copies ran while one was open for 27% -> 0% of each run, Pallas kernels for 0% -> 0%
where the time goes in v1:
time: 344 us; the launch traced here: 342 us
  Pallas kernels  322 us (94%)
  other arithmetic  9.72 us (3%)
  local copies, waits for them, and re-layouts  9.5 us (3%)
    pallas_call x1, Pallas kernels, fused_step(): pl.pallas_call(functools.partial(step_kernel, NZ), out_shape=(jax.ShapeDt...  322 us
    unnamed x57, local copies, waits for them, and re-layouts  9.5 us

profile of v1, /device:TPU:0, one launch (start us, length us, event | category | flops | bytes accessed | tf_op | source)
XLA Modules:
  0.0 342.5 jit_solution(5817941634558401766)
XLA Ops:
  0.7 0.0 copy-start.20
  0.7 0.0 copy-start.24
  0.7 0.0 copy-start.23
  0.7 322.4 %shard_map.385 = (bf16[1,256,768]{2,1,0:T(8,128)(2,1)}, bf16[1,256,768]{2,1,0:T(8,128)(2,1)}, f32[2,4,24,768]{3,2,1,0:T(8,128)}, f32[2,24,3072]{2,1,0:T(8,128)},...) custom-call(bf16[1,256,768]{2,1,0:T(8,128)(2,1)} %x_in.1, bf16[1,256,768]{2,1,0:T(8,128)(2,1)} %cot_in.1, ...), custom_call_target="tpu_custom_call" | custom-call | tf_op jit(solution)/shard_map/pallas_call | solution.py:1135
  323.2 0.0 copy-start.19
  323.2 0.0 copy-start.22
  323.2 0.0 copy-start.15
  323.2 0.0 copy-start.17
  323.2 0.0 copy-done.20
  323.2 0.0 copy-done.24
  323.2 0.6 copy-done.22
  323.8 0.6 fusion
  324.4 0.6 copy-done.21
  324.9 0.0 copy-done.23
  324.9 0.6 add_multiply_fusion.4
  325.5 0.0 copy-done.19
  325.5 0.6 fusion.1
  326.1 0.1 copy-done.18
  326.2 0.6 add_multiply_fusion.3
  326.8 2.6 fusion.2
  329.4 0.0 copy-start.6
  329.4 0.0 copy-start.9
  329.4 0.9 add_multiply_fusion
  330.3 0.1 copy-done
  330.4 0.5 copy-done.4
  330.9 0.2 copy-done.6
  331.1 0.2 copy-done.9
  331.2 1.1 fusion.3
  332.3 0.0 copy-done.10
  332.4 0.0 copy-start.11
  332.4 0.9 add_multiply_fusion.1
  333.2 0.1 copy-done.1
  333.3 0.5 copy-done.5
  333.8 0.2 copy-done.7
  334.0 0.2 copy-done.11
  334.2 1.1 fusion.4
  335.3 0.9 add_multiply_fusion.2
  336.2 0.1 copy-done.2
  336.3 0.3 copy-done.14
  336.5 0.7 copy.52
  337.3 0.4 copy-done.13
  337.7 0.7 copy.53
  338.4 0.8 copy.54
  339.2 0.8 copy.55
  340.1 0.5 copy-done.3
  340.5 0.8 copy.56
  341.3 0.6 copy.57
  341.9 0.6 copy.58
  (20 shorter events, 0.0 us)
Async XLA Ops:
  0.7 322.5 %copy-start.20 = (f32[2,96]{1,0:T(2,128)S(1)}, f32[2,96]{1,0:T(2,128)}, u32[]{:S(2)}) copy-start(f32[2,96]{1,0:T(2,128)} %hb.1) | copy-start | bytes 2308
  0.7 322.5 %copy-start.24 = (f32[2,96]{1,0:T(2,128)S(1)}, f32[2,96]{1,0:T(2,128)}, u32[]{:S(2)}) copy-start(f32[2,96]{1,0:T(2,128)} %param.34) | copy-start | bytes 2308
  0.7 324.3 %copy-start.23 = (f32[2,96]{1,0:T(2,128)S(1)}, f32[2,96]{1,0:T(2,128)}, u32[]{:S(2)}) copy-start(f32[2,96]{1,0:T(2,128)} %param.35) | copy-start | bytes 2308
  323.2 2.4 copy-start.19
  323.2 0.6 copy-start.22
  323.2 2.3 copy-start.15
  323.2 2.3 copy-start.17
  324.4 0.6 copy-start.21
  325.5 0.7 copy-start.18
  326.1 0.7 copy-start.16
  326.8 2.6 copy-start.8
  329.4 1.0 copy-start
  329.4 1.5 copy-start.4
  329.4 1.7 copy-start.6
  329.4 1.8 copy-start.9
  331.2 1.1 copy-start.10
  332.3 1.0 copy-start.1
  332.3 1.5 copy-start.5
  332.3 1.7 copy-start.7
  332.4 1.8 copy-start.11
  334.2 1.1 copy-start.12
  335.3 1.0 copy-start.2
  335.3 1.3 copy-start.14
  336.5 1.1 copy-start.13
  339.2 1.3 copy-start.3

commit v2 on v1

--- a/solution.py
+++ b/solution.py
@@ -18,7 +18,7 @@
 DECAY_RATE = 0.0001
 AVERAGE_RATE = 0.5
 LEARN_BASE = 0.1
-VMEM_BYTES = 66500000
+VMEM_BYTES = 66900000
 
 
 def as_sent(shard):
@@ -378,9 +378,9 @@
 def step_kernel(NZ, x_in, cot_in, lens, aw, uw, dw, lv, hb, *rest):
     (out, gin, gA, gU, gD, gV, gB) = rest[:7]
     (
-        w1, w2, w3, w4, stg, rsl, gm, a, b, qh, kk, vv, kT, vT, oh, ofull, goh, gos, gpo, lse,
-        x1, xs, hact, gpb, segc, segr, facc, gq, gw1, gw2, gw3, gw4, gw5, xl1, xl2, xl3, xl4, xl5,
-        zl1, zl2, zl3, zl4, zl5, ps1, ps2, ps3, ps5, pl1, pl2, pl3, pl5, tt, V, vg, snd, rcv,
+        w1, w2, w3, w4, stg, rsl, gm, a, b, qh, kk, vv, kT, vT, oh, ofull, goh, gpo, lse,
+        x1, xs, xs_out, hact, gpb, segc, segr, facc, gq, gw1, gw2, gw3, gw4, gw5, xl1, xl2, xl3, xl4, xl5,
+        zl1, zl2, zl3, zl4, zl5, cl, ps1, ps2, ps3, ps5, pl1, pl2, pl3, pl5, tt, V, vg, snd, rcv,
         credx, credz,
     ) = rest[7:]
     W = {1: w1, 2: w2, 3: w3, 4: w4}
@@ -394,6 +394,7 @@
     R = aw.shape[2]
     CH = R * S
     DP = NZ * 2
+    ORDER = (1, NZ - 1) + tuple(range(2, NZ - 1))
     FJ = hb.shape[1]
 
     d = lax.axis_index("dp")
@@ -404,6 +405,8 @@
 
     def xor(k):
         return ((y + k // 2) % 2) * 2 + (c + k % 2) % 2
+
+    member = xor
 
     def dev(dd, ss):
         return {"dp": dd, "seq": ss}
@@ -468,41 +471,59 @@
 
     ag_sems = {}
 
-    def ag_start(g, l):
-        zi, xi = sems(NZ), sems(NZ)
-        ag_sems[g, l] = (zi, xi)
-        own = W[g].at[l, chunk(d)]
-        for dz in range(1, NZ):
-            rc(own, own, zdev(dz), zi + dz).start()
-            sent_weights.append((g, zi + dz))
-
-    def ag_forward(g, l):
-        zi, xi = ag_sems[g, l]
+    def part(g, dd):
+        if g == 2:
+            return pl.ds(pl.multiple_of(dd * CH + c * (CH // 2), 16), CH // 2)
+        return chunk(dd)
+
+    def ag_z(g, l, *steps):
+        if (g, l) not in ag_sems:
+            ag_sems[g, l] = sems(2 * NZ if g != 2 else 2 * NZ + DP)
+        i = ag_sems[g, l]
+        own = W[g].at[l, part(g, d)]
+        for dz in steps or ORDER:
+            rc(own, own, zdev(dz), i + dz).start()
+            sent_weights.append((g, i + dz))
+
+    def ag_x(g, l, *steps):
+        i = ag_sems[g, l]
+        for dz in steps:
+            ref = W[g].at[l, part(g, ((z - dz + NZ) % NZ) * 2 + x)]
+            if dz:
+                rc(ref, ref, zdev(dz), i + dz).wait_recv()
+            rc(ref, ref, x_peer, i + NZ + dz).start()
+            sent_weights.append((g, i + NZ + dz))
+
+    def ag_done(g, l):
+        i = ag_sems[g, l] + NZ
         for dz in range(NZ):
-            part = W[g].at[l, chunk(((z - dz + NZ) % NZ) * 2 + x)]
-            if dz:
-                rc(part, part, zdev(dz), zi + dz).wait_recv()
-            rc(part, part, x_peer, xi + dz).start()
-            sent_weights.append((g, xi + dz))
-
-    def ag_done(g, l):
-        xi = ag_sems[g, l][1]
-        for dz in range(NZ):
-            part = W[g].at[l, chunk(dz)]
-            rc(part, part, x_peer, xi + dz).wait_recv()
+            ref = W[g].at[l, part(g, dz)]
+            rc(ref, ref, x_peer, i + dz).wait_recv()
+
+    def ag_core(g, l, start):
+        i = ag_sems[g, l] + 2 * NZ
+        for k in range(1, DP):
+            ref = W[g].at[l, part(g, (d + k) % DP)]
+            copy = rc(ref, ref, core_peer, i + k)
+            if start:
+                copy.start()
+                sent_weights.append((g, i + k))
+            else:
+                copy.wait_recv()
 
     red_sems = {}
 
-    def x_copies(g, l):
-        i = red_sems[g, l]
-        return [rc(GW[g].at[chunk(zi * 2 + xp)], XL[g].at[zi], x_peer, i + zi) for zi in range(NZ)]
-
-    def z_copies(g, l):
-        i = red_sems[g, l] + NZ
-        return [
-            rc(GW[g].at[chunk(((z + dz) % NZ) * 2 + x)], ZL[g].at[dz - 1], zdev(dz), i + dz)
-            for dz in range(1, NZ)
-        ]
+    def x_copy(g, l, dz):
+        zi = (z + dz) % NZ
+        return rc(
+            GW[g].at[part(g, zi * 2 + xp)], XL[g].at[dz], x_peer, red_sems[g, l] + dz
+        )
+
+    def z_copy(g, l, dz):
+        return rc(
+            GW[g].at[part(g, ((z + dz) % NZ) * 2 + x)], ZL[g].at[dz - 1], zdev(dz),
+            red_sems[g, l] + NZ + dz,
+        )
 
     def s_copies(g, l):
         i = red_sems[g, l] + 2 * NZ
@@ -511,32 +532,73 @@
             for ds in range(1, S)
         ]
 
+    def half_copies(l, action):
+        i = red_sems[2, l] + 2 * NZ
+        for k in range(2):
+            to = 2 * c + k
+            copy = pltpu.make_async_remote_copy(
+                src_ref=PS[2].at[k], dst_ref=PL[2].at[y], send_sem=snd.at[i + k],
+                recv_sem=rcv.at[i + y], device_id=dev(d, to), device_id_type=MESH,
+            )
+            pl.when(to != s)(functools.partial(action, copy))
+
+    def half_arrivals(l):
+        i = red_sems[2, l] + 2 * NZ
+        for k in range(2):
+            copy = rc(PL[2].at[k], PL[2].at[k], core_peer, i + k)
+            pl.when(2 * k + s // 2 != s)(lambda copy=copy: copy.wait_recv())
+
+    def core_copies(l):
+        i = red_sems[2, l] + 3 * NZ
+        other = CH // 2 * (1 - c)
+        return [
+            rc(
+                gw2.at[pl.ds(pl.multiple_of(k * CH + other, 16), CH // 2)], cl.at[k], core_peer, i + k
+            )
+            for k in range(DP)
+        ]
+
+    def red_core(l):
+        red_sems[2, l] = sems(3 * NZ + DP)
+        for copy in core_copies(l):
+            copy.start()
+
     def red_x(g, l):
         if l == 0 and g != 5:
             pl.semaphore_wait(credx.at[g], 1)
-        red_sems[g, l] = sems(2 * NZ + S)
-        for copy in x_copies(g, l):
-            copy.start()
-
-    def red_z(g, l):
-        for zi, copy in enumerate(x_copies(g, l)):
-            copy.wait_recv()
-            mine = chunk(zi * 2 + x)
-            GW[g][mine] = (GW[g][mine].astype(F32) + XL[g][zi].astype(F32)).astype(BF16)
-        if l == 1 and g != 5:
-            pl.semaphore_signal(credx.at[g], 1, device_id=x_peer, device_id_type=MESH)
-        if l == 0 and g != 5:
-            pl.semaphore_wait(credz.at[g], NZ - 1)
-        for copy in z_copies(g, l):
-            copy.start()
+        if g == 2:
+            for k, copy in enumerate(core_copies(l)):
+                copy.wait_recv()
+                gw2[part(2, k)] = (gw2[part(2, k)].astype(F32) + cl[k].astype(F32)).astype(BF16)
+        else:
+            red_sems[g, l] = sems(2 * NZ + S)
+        for dz in ORDER + (0,):
+            x_copy(g, l, dz).start()
+
+    def red_z(g, l, *steps):
+        for dz in steps or ORDER + (0,):
+            x_copy(g, l, dz).wait_recv()
+            mine = part(g, ((z + dz) % NZ) * 2 + x)
+            GW[g][mine] = (GW[g][mine].astype(F32) + XL[g][dz].astype(F32)).astype(BF16)
+            if dz:
+                if l == 0 and g != 5 and dz == ORDER[0]:
+                    pl.semaphore_wait(credz.at[g], NZ - 1)
+                z_copy(g, l, dz).start()
+            elif l == 1 and g != 5:
+                pl.semaphore_signal(credx.at[g], 1, device_id=x_peer, device_id_type=MESH)
 
     def red_sum(g, l):
-        total = GW[g][chunk(d)].astype(F32)
-        for k, copy in enumerate(z_copies(g, l)):
-            copy.wait_recv()
-            total = total + ZL[g][k].astype(F32)
-        for copy in x_copies(g, l) + z_copies(g, l):
-            copy.wait_send()
+        total = GW[g][part(g, d)].astype(F32)
+        for dz in ORDER:
+            z_copy(g, l, dz).wait_recv()
+            total = total + ZL[g][dz - 1].astype(F32)
+        for dz in ORDER:
+            z_copy(g, l, dz).wait_send()
+        for dz in range(NZ):
+            x_copy(g, l, dz).wait_send()
+        if g == 2:
+            for copy in core_copies(l):
+                copy.wait_send()
         if l == 1 and g != 5:
             for dz in range(1, NZ):
                 pl.semaphore_signal(credz.at[g], 1, device_id=zdev(dz), device_id_type=MESH)
@@ -546,16 +608,27 @@
         if g == 5:
             tt[0:CH, :] = total
         wide = total.shape[1]
-        for k in range(S):
-            piece = jnp.concatenate(
-                [total[R * k : R * (k + 1)], jnp.zeros((PS[g].shape[1] - R, wide), F32)], axis=0
-            )
+        pad = jnp.zeros((PS[g].shape[1] - R, wide), F32)
+        for k in range(2 if g == 2 else S):
+            piece = jnp.concatenate([total[R * k : R * (k + 1)], pad], axis=0)
             PS[g][k] = piece.astype(BF16)
+        if g == 2:
+            half_copies(l, lambda copy: copy.start())
+
+            @pl.when(s // 2 == c)
+            def _():
+                PL[2][y] = PS[2][y]
+            return
         PL[g][s] = PS[g][s]
         for copy in s_copies(g, l):
             copy.start()
 
     def red_write(g, l):
+        if g == 2:
+            half_arrivals(l)
+            gA[l, 3] = PL[2][0].astype(F32)[0:R] + PL[2][1].astype(F32)[0:R]
+            half_copies(l, lambda copy: copy.wait_send())
+            return
         for copy in s_copies(g, l):
             copy.wait_recv()
         parts = [PL[g][k].astype(F32)[0:R] for k in range(S)]
@@ -565,8 +638,6 @@
                 [q for p in parts for q in (p[:, 256:384], p[:, 192:256])], axis=1
             )
             gA[l, 2] = jnp.concatenate([p[:, 384:576] for p in parts], axis=1)
-        elif g == 2:
-            gA[l, 3] = parts[0] + parts[1] + parts[2] + parts[3]
         elif g == 3:
             gU[l] = jnp.concatenate(
                 [parts[k][:, FJ * i : FJ * (i + 1)] for i in range(DP) for k in range(S)], axis=1
@@ -584,34 +655,44 @@
     parity = [0]
 
     class Scatter:
-        def __init__(self):
+        def __init__(self, shifted=False):
             i = sems(3)
             base = parity[0] * 3
             parity[0] = 1 - parity[0]
             self.base = base
+            self.shifted = shifted
+            self.y_at = 3 * T if shifted else 2 * T
             self.r0 = rc(stg.at[0:T], rsl.at[base], core_peer, i)
             self.r1 = rc(stg.at[T : 2 * T], rsl.at[base + 1], core_peer, i + 1)
-            self.r2 = rc(stg.at[2 * T : 3 * T], rsl.at[base + 2], y_peer, i + 2)
-
-        def send_core(self, j):
-            k = 0 if j == 3 else 1
-            stg[T * k : T * (k + 1)] = facc[T * j : T * (j + 1)].astype(BF16)
-            (self.r0 if j == 3 else self.r1).start()
+            self.r2 = rc(stg.at[self.y_at : self.y_at + T], rsl.at[base + 2], y_peer, i + 2)
+
+        def slot(self, k):
+            return rows(1 + k - 2 * (k // 3)) if self.shifted else rows(k)
+
+        def send_core(self, k):
+            at = 0 if k == 3 else 1
+            stg[T * at : T * (at + 1)] = facc[self.slot(k)].astype(BF16)
+            (self.r0 if k == 3 else self.r1).start()
 
         def send_y(self):
             self.r0.wait_recv()
-            stg[2 * T : 3 * T] = (
-                facc[2 * T : 3 * T] + rsl[self.base].astype(F32)
+            stg[self.y_at : self.y_at + T] = (
+                facc[self.slot(2)] + rsl[self.base].astype(F32)
             ).astype(BF16)
             self.r2.start()
 
-        def finish(self):
+        def core_sent(self):
+            self.r0.wait_send()
+            self.r1.wait_send()
+
+        def received(self):
             self.r1.wait_recv()
             self.r2.wait_recv()
-            total = facc[0:T] + rsl[self.base + 1].astype(F32) + rsl[self.base + 2].astype(F32)
-            for copy in (self.r0, self.r1, self.r2):
-                copy.wait_send()
-            return total
+            self.r2.wait_send()
+            return rsl[self.base + 1].astype(F32) + rsl[self.base + 2].astype(F32)
+
+        def finish(self):
+            return facc[self.slot(0)] + self.received()
 
     barrier = pltpu.get_barrier_semaphore()
     greeted = [core_peer, y_peer, dev(d, xor(3)), x_peer] + [zdev(dz) for dz in range(1, NZ)]
@@ -640,22 +721,6 @@
                 )
             )
         stg[144 * k : 144 * k + 48, 0:640] = jnp.concatenate(two, axis=0).astype(BF16)
-    gm[0, rows(s)] = x_in[0]
-
-    pl.semaphore_wait(barrier, len(greeted))
-
-    def piece_rows(k):
-        return pl.multiple_of(k * 144, 16)
-
-    i = sems(S)
-    pieces1 = []
-    for ds in (2, 3, 1):
-        to = xor(ds)
-        copy = rc(stg.at[pl.ds(piece_rows(to), 48), 0:640], rsl.at[s, 0:48, 0:640], dev(d, to), i + ds)
-        copy.start()
-        pieces1.append(copy)
-    gather_x = Gather(gm.at[0])
-    gather_x.start()
     for k in range(S):
         two = [
             jnp.concatenate(
@@ -665,21 +730,38 @@
         ]
         stg[144 * k + 48 : 144 * k + 96, :] = jnp.concatenate([aw[0, 3], aw[1, 3]], axis=0).astype(BF16)
         stg[144 * k + 96 : 144 * k + 144, :] = jnp.concatenate(two, axis=0).astype(BF16)
-    i = sems(S)
-    pieces2 = []
-    for ds in (2, 3, 1):
-        to = xor(ds)
-        copy = rc(
-            stg.at[pl.ds(pl.multiple_of(piece_rows(to) + 48, 16), 96), :],
-            rsl.at[s, 48:144, :], dev(d, to), i + ds,
-        )
-        copy.start()
-        pieces2.append(copy)
+    gm[0, rows(s)] = x_in[0]
+
+    pl.semaphore_wait(barrier, len(greeted))
+
+    def piece_rows(k):
+        return pl.multiple_of(k * 144, 16)
+
+    def send_pieces(source, target):
+        i = sems(S)
+        copies = []
+        for ds in (2, 3, 1):
+            to = xor(ds)
+            copies.append(rc(source(to), target, dev(d, to), i + ds))
+        for copy in copies:
+            copy.start()
+        return copies
+
+    pieces1 = send_pieces(
+        lambda to: stg.at[pl.ds(piece_rows(to), 48), 0:640], rsl.at[s, 0:48, 0:640]
+    )
+    pieces2 = send_pieces(
+        lambda to: stg.at[pl.ds(pl.multiple_of(piece_rows(to) + 48, 16), 96), :], rsl.at[s, 48:144, :]
+    )
+    gather_x = Gather(gm.at[0])
+    gather_x.start()
+    w4[0, chunk(d)] = dw[0].astype(BF16)
+    ag_z(4, 0, *ORDER[:2])
+    ag_x(4, 0, 0)
+    w4[1, chunk(d)] = dw[1].astype(BF16)
     rsl[s, 0:48, 0:640] = stg[pl.ds(piece_rows(s), 48), 0:640]
     rsl[s, 48:144, :] = stg[pl.ds(pl.multiple_of(piece_rows(s) + 48, 16), 96), :]
     vg[...] = jnp.zeros_like(vg)
-    for l in range(2):
-        w4[l, chunk(d)] = dw[l].astype(BF16)
     for copy in pieces1:
         copy.wait_recv()
     got = [rsl[k, 0:48, 0:640].astype(F32) for k in range(S)]
@@ -688,7 +770,9 @@
         if l == 0:
             full = jnp.concatenate([full[:, 0:512], full[:, 512:640] + bias_cols], axis=1)
         w1[l, chunk(d)] = full.astype(BF16)
-    ag_start(1, 0)
+    ag_z(1, 0)
+    ag_x(1, 0, 0)
+    ag_x(4, 0, ORDER[0])
 
     bounds = []
     running = jnp.int32(0)
@@ -707,19 +791,25 @@
     segr[...] = segments((8, N), 1)
     segc[...] = segments((N, 128), 0)
 
+    ag_x(1, 0, ORDER[0])
     for copy in pieces2:
         copy.wait_recv()
     for g, at in ((2, 48), (3, 96)):
         got = [rsl[k, at : at + 48, :].astype(F32) for k in range(S)]
         for l in range(2):
             W[g][l, chunk(d)] = jnp.concatenate(
-                [part[R * l : R * (l + 1)] for part in got], axis=0
+                [piece[R * l : R * (l + 1)] for piece in got], axis=0
             ).astype(BF16)
     for copy in pieces1 + pieces2:
         copy.wait_send()
-    ag_start(2, 0)
-    ag_forward(1, 0)
-    ag_start(3, 0)
+    ag_x(1, 0, ORDER[1])
+    ag_x(1, 0, *ORDER[2:])
+    ag_z(2, 0)
+    ag_z(3, 0)
+    ag_z(4, 0, *ORDER[2:])
+    ag_x(2, 0, 0)
+    ag_x(4, 0, ORDER[1])
+    ag_x(3, 0, 0)
     gather_x.core()
     gather_x.forward()
     gm[1, rows(s)] = cot_in[0]
@@ -782,11 +872,17 @@
         return q, k
 
     def attend(l, points):
+        i0 = sems(S)
+        order = (2, 3, 1)
+        copies = [
+            rc(oh.at[l, rows(xor(k))], goh.at[rows(s)], dev(d, xor(k)), i0 + k) for k in order
+        ]
+
         @pl.loop(0, N // QBLOCK)
-        def _(qb):
+        def _(i):
             for at, action in points.items():
-                pl.when(qb == at)(action)
-            q, k = query_block(qb)
+                pl.when(i == at)(action)
+            q, k = query_block(member((2 + i) * (1 - i // 2) + (3 - i) * (i // 2)))
             allowed = jnp.concatenate([segc[k, :]] * 2, axis=1) == segr[0:1, q]
             parts = []
             for h in range(3):
@@ -798,15 +894,23 @@
                 parts.append(nn(vT[h // 2, :, k], grown.astype(BF16)) / total)
             oh[l, q, 0:128] = jnp.transpose(jnp.where(low_rows, parts[0], parts[1])).astype(BF16)
             oh[l, q, 128:256] = jnp.transpose(parts[2]).astype(BF16)
-
-    def attend_grad(l, points):
+            for at in range(3):
+                pl.when(i == at)(copies[at].start)
+
+        goh[rows(s)] = oh[l, rows(s)]
+        pending.extend(copies)
+        return copies
+
+    def attend_grad(l, copies, points):
         facc[:, 0:512] = jnp.zeros((N, 512), F32)
 
         @pl.loop(0, N // QBLOCK)
-        def _(qb):
+        def _(i):
+            for at in range(1, S):
+                pl.when(i == at)(copies[at].wait)
             for at, action in points.items():
-                pl.when(qb == at)(action)
-            q, k = query_block(qb)
+                pl.when(i == at)(action)
+            q, k = query_block(member(i))
             allowed = jnp.concatenate([segc[k, :]] * 2, axis=1) == segr[0:1, q]
             tiles = [goh[q, 0:128], goh[q, 128:256]]
             inner = [
@@ -849,40 +953,47 @@
 
     def exchange(source, target):
         i = sems(S)
-        copies = []
+        copies = {}
         for ds in (2, 3, 1):
             to = xor(ds)
-            part = source(to)
-            copies.append(rc(part, target(s), dev(d, to), i + ds))
-        for copy in copies:
-            copy.start()
+            copies[ds] = rc(source(to), target(s), dev(d, to), i + ds)
+            copies[ds].start()
         return copies
 
-    def mlp_forward(l, gather):
-        scatter = Scatter()
-
+    def mlp_up(l, gather, points):
         @pl.loop(0, S)
         def _(k):
             pl.when(k == 1)(gather.core)
             pl.when(k == 2)(gather.forward)
             pl.when(k == 3)(gather.last)
-            r = rows(((y + k // 2) % 2) * 2 + (c + k % 2) % 2)
+            for at, action in points.items():
+                pl.when(k == at)(action)
+            r = rows(member(k))
             pre = nn(b[l, r], w3[l]) + V[16 + l : 17 + l, :]
             cdf = 0.5 * (1.0 + lax.erf(pre * 0.7071067811865476))
             density = jnp.exp(-0.5 * pre * pre) * 0.3989422804014327
-            act = (pre * cdf).astype(BF16)
-            hact[l, r] = act
+            hact[l, r] = (pre * cdf).astype(BF16)
             gpb[l, r] = (cdf + pre * density).astype(BF16)
-            facc[rows(k)] = nn(act, w4[l])
+
+        gather.done()
+
+    def scatter_rows(term, shifted=False, across=True):
+        scatter = Scatter(shifted)
+
+        @pl.loop(0, S)
+        def _(i):
+            k = S - 1 - i
+            facc[scatter.slot(k)] = term(rows(member(k)))
             pl.when(k == 1)(lambda: scatter.send_core(1))
             pl.when(k == 3)(lambda: scatter.send_core(3))
-
-        gather.done()
-        scatter.send_y()
+            if across:
+                pl.when(k == 2)(scatter.send_y)
+
         return scatter
 
-    def mlp_backward(l, gather):
+    def mlp_backward(l, gather, points):
         scatter = Scatter()
+
         @pl.loop(0, S, init_carry=jnp.zeros((1, D), F32))
         def bias_grad(i, carry):
             if gather is None:
@@ -892,7 +1003,9 @@
                 pl.when(k == 1)(gather.core)
                 pl.when(k == 2)(gather.forward)
                 pl.when(k == 3)(gather.last)
-            r = rows(((y + k // 2) % 2) * 2 + (c + k % 2) % 2)
+            for at, action in points.items():
+                pl.when(i == at)(action)
+            r = rows(member(k))
             grad_act = nt(gm[l, r], w4[l])
             grad_pre = (grad_act * gpb[l, r].astype(F32)).astype(BF16)
             gpb[l, r] = grad_pre
@@ -915,150 +1028,153 @@
             m = pl.ds(pl.multiple_of(i * 384, 384), 384)
             GW[g][m, :] = tn(left(m), right()).astype(BF16)
 
-    def heads_input_grad(l):
-        scatter = Scatter()
-
-        @pl.loop(0, S)
-        def _(i):
-            k = S - 1 - i
-            r = rows(((y + k // 2) % 2) * 2 + (c + k % 2) % 2)
-            facc[rows(k)] = nt(gq[r], w1[l])
-            pl.when(k == 1)(lambda: scatter.send_core(1))
-            pl.when(k == 3)(lambda: scatter.send_core(3))
-            pl.when(k == 2)(scatter.send_y)
-
-        return scatter
-
     def column(values):
         return jnp.sum(values.astype(F32), axis=0, keepdims=True)
 
     gather_cot = Gather(gm.at[1])
-    gather_b = {}
-    later = [
-        lambda: (ag_forward(2, 0), ag_start(4, 0)),
-        lambda: (ag_forward(3, 0), ag_start(1, 1)),
-        lambda: (ag_forward(4, 0), ag_start(2, 1)),
-        lambda: (ag_forward(1, 1), ag_start(3, 1)),
-        lambda: (ag_forward(2, 1), ag_start(4, 1)),
-        lambda: ag_forward(3, 1),
-        lambda: ag_forward(4, 1),
-    ]
-
-    def do_later():
-        later.pop(0)()
-
+    last = ORDER[2:]
     for l in range(2):
         project_heads(l)
         if l == 0:
             gather_cot.start()
-        do_later()
-        if l == 0:
-            def point():
-                do_later()
-                gather_cot.core()
-                gather_cot.forward()
-            attend(l, {2: point})
-            gather_cot.last()
-            gather_cot.done()
+            ag_x(2, 0, *ORDER[:2])
+
+            def core_stage():
+                ag_done(2, 0)
+                ag_core(2, 0, True)
+                ag_x(3, 0, ORDER[0])
+
+            copies = attend(0, {1: lambda: ag_x(2, 0, *last), 3: core_stage})
         else:
-            attend(l, {2: do_later})
-        copies = exchange(lambda to: oh.at[l, rows(to)], lambda me: goh.at[rows(me)])
-        goh[rows(s)] = oh[l, rows(s)]
-        pending.extend(copies)
-        ag_done(2, l)
+
+            def core_stage():
+                ag_done(2, 1)
+                ag_core(2, 1, True)
+
+            copies = attend(1, {1: lambda: ag_x(3, 1, *last), 2: core_stage, 3: lambda: ag_x(4, 1, 0, ORDER[0])})
         for copy in copies:
             copy.wait_recv()
-        ofull[l] = jnp.concatenate([goh[T * k : T * (k + 1)].astype(F32)[:, 0:192] for k in range(S)], axis=1).astype(BF16)
+        ag_core(2, l, False)
+        ofull[l] = jnp.concatenate(
+            [goh[T * k : T * (k + 1)].astype(F32)[:, 0:192] for k in range(S)], axis=1
+        ).astype(BF16)
         before = x_in[0].astype(F32) if l == 0 else xs[...]
         middle = before + (nn(ofull[l], w2[l]) + vec(l, 4))
         x1[l] = middle
         unit, _ = norm_parts(middle)
         b[l, rows(s)] = (unit * vec(l, 5) + vec(l, 6)).astype(BF16)
-        gather_b[l] = Gather(b.at[l])
-        gather_b[l].start()
+        gather_b = Gather(b.at[l])
+        gather_b.start()
         if l == 0:
-            do_later()
+            gather_cot.core()
+            gather_cot.forward()
+            ag_z(1, 1)
+            ag_z(2, 1)
+            ag_x(3, 0, *ORDER[1:])
+            gather_cot.last()
+            gather_cot.done()
+        else:
+            ag_x(4, 1, ORDER[1])
         ag_done(3, l)
+        if l == 0:
+            mlp_up(0, gather_b, {1: lambda: ag_x(4, 0, *last)})
+            ag_z(3, 1)
+            ag_z(4, 1)
+        else:
+            mlp_up(1, gather_b, {2: lambda: ag_x(4, 1, *last)})
         ag_done(4, l)
-        scatter = mlp_forward(l, gather_b[l])
-        if l == 0:
-            do_later()
-        after = x1[l] + (scatter.finish() + vec(l, 7))
+        if l == 1:
+            break
+        scatter = scatter_rows(lambda r: nn(hact[0, r], w4[0]))
+        ag_x(1, 1, 0, *ORDER)
+        after = x1[0] + (scatter.finish() + vec(0, 7))
+        scatter.core_sent()
         flush()
-        if l == 0:
-            xs[...] = after
-            unit, _ = norm_parts(after)
-            a[1, rows(s)] = (unit * vec(1, 0) + vec(1, 1)).astype(BF16)
-            gather_a = Gather(a.at[1])
-            gather_a.start()
-            do_later()
-            ag_done(1, 1)
-            gather_a.core()
-            gather_a.forward()
-            gather_a.last()
-            gather_a.done()
-            do_later()
-            later.insert(0, lambda: None)
-        else:
-            out[0] = after.astype(BF16)
-
-    grad = cot_in[0].astype(F32)
+        xs[...] = after
+        unit, _ = norm_parts(after)
+        a[1, rows(s)] = (unit * vec(1, 0) + vec(1, 1)).astype(BF16)
+        gather_a = Gather(a.at[1])
+        gather_a.start()
+        ag_x(2, 1, 0, *ORDER)
+        ag_x(3, 1, 0, ORDER[0])
+        ag_done(1, 1)
+        gather_a.core()
+        gather_a.forward()
+        ag_x(3, 1, ORDER[1])
+        gather_a.last()
+        gather_a.done()
+
     gather = None
     for l in (1, 0):
         first = l == 1
-        scatter = mlp_backward(l, gather)
-        if not first:
-            red_write(2, 1)
-            red_write(3, 1)
-            red_sum(1, 1)
+        if first:
+            scatter = mlp_backward(1, None, {})
+        else:
+            scatter = mlp_backward(0, gather, {})
         vg[16 * l + 7 : 16 * l + 8, :] = column(gm[l, rows(s)])
         weight_grad(4, lambda m: hact[l, :, m], lambda: gm[l])
         red_x(4, l)
         weight_grad(3, lambda m: b[l, :, m], lambda: gpb[l])
         red_x(3, l)
+        if first:
+            scatter.core_sent()
+            scatter_out = scatter_rows(lambda r: nn(hact[1, r], w4[1]), True, False)
+            red_z(4, 1, ORDER[0])
+        else:
+            red_sum(2, 1)
+            red_write(3, 1)
+            red_sum(1, 1)
+            red_z(4, 0, ORDER[0])
         grad_b = scatter.finish()
         grad_x1, gain, shift = norm_back(x1[l], grad_b, vec(l, 5))
+        grad_x1 = grad_x1 + (cot_in[0].astype(F32) if first else xs[...])
         if first:
-            grad_x1 = grad_x1 + cot_in[0].astype(F32)
-        else:
-            grad_x1 = grad_x1 + xs[...]
+            xs_out[...] = x1[1] + facc[scatter_out.slot(0)]
         x1[l] = grad_x1
-        vg[16 * l + 5 : 16 * l + 6, :] = gain
-        vg[16 * l + 6 : 16 * l + 7, :] = shift
         gpo[...] = grad_x1.astype(BF16)
-        vg[16 * l + 4 : 16 * l + 5, :] = column(gpo[...])
         flush()
         back = nt(gpo[...], w2[l])
         for k in range(S):
-            gos[k] = jnp.concatenate(
+            gq[rows(k), 0:256] = jnp.concatenate(
                 [back[:, 192 * k : 192 * (k + 1)], jnp.zeros((T, 64), F32)], axis=1
             ).astype(BF16)
-        copies = exchange(lambda to: gos.at[to], lambda me: goh.at[rows(me)])
-        goh[rows(s)] = gos[s]
-        pending.extend(copies)
-        if not first:
-            red_write(1, 1)
-        weight_grad(2, lambda m: ofull[l, :, m], lambda: gpo[...])
-        red_x(2, l)
-        red_z(4, l)
-        for copy in copies:
-            copy.wait_recv()
-
-        def point_a():
-            red_z(3, l)
-
-        def point_b():
-            red_z(2, l)
-
-        attend_grad(l, {2: point_a, 3: point_b})
+        copies = exchange(lambda to: gq.at[rows(to), 0:256], lambda me: goh.at[rows(me)])
+        goh[rows(s)] = gq[rows(s), 0:256]
+        vg[16 * l + 5 : 16 * l + 6, :] = gain
+        vg[16 * l + 6 : 16 * l + 7, :] = shift
+        vg[16 * l + 4 : 16 * l + 5, :] = column(gpo[...])
+        if first:
+            scatter_out.send_y()
+        red_z(4, l, ORDER[1])
+        attend_grad(
+            l,
+            copies,
+            {
+                1: lambda: red_z(4, l, *last),
+                2: lambda: (red_z(4, l, 0), None if first else red_write(1, 1))[1],
+                3: lambda: red_z(3, l, ORDER[0]),
+            },
+        )
         sums = column(gq[...])
         vg[16 * l + 2 : 16 * l + 3, :] = at_heads(sums[:, 0:192])
         vg[16 * l + 3 : 16 * l + 4, :] = at_heads(sums[:, 384:576])
-        scatter = heads_input_grad(l)
+        if first:
+            out[0] = (xs_out[...] + (scatter_out.received() + vec(1, 7))).astype(BF16)
+            scatter_out.core_sent()
+        else:
+            scatter.core_sent()
+        scatter = scatter_rows(lambda r: nt(gq[r], w1[l]))
         weight_grad(1, lambda m: a[l, :, m], lambda: gq[...])
         red_x(1, l)
-        red_sum(4, l)
+        weight_grad(2, lambda m: ofull[l, :, m], lambda: gpo[...])
+        red_core(l)
+        red_z(3, l, ORDER[1])
+        red_x(2, l)
+        if not first:
+            red_write(2, 1)
+        red_z(3, l, *last)
         grad_a = scatter.finish()
+        scatter.core_sent()
         before = xs[...] if first else x_in[0].astype(F32)
         grad, gain, shift = norm_back(before, grad_a, vec(l, 0))
         grad = grad + x1[l]
@@ -1070,28 +1186,33 @@
             gm[0, rows(s)] = grad.astype(BF16)
             gather = Gather(gm.at[0])
             gather.start()
-            red_sum(3, 1)
-            red_sum(2, 1)
-            red_z(1, 1)
         else:
             gin[0] = grad.astype(BF16)
-
-    gw5[...] = jnp.transpose(vg[...]).astype(BF16)
-    red_x(5, 0)
+            gw5[...] = jnp.transpose(vg[...]).astype(BF16)
+            red_x(5, 0)
+        red_z(3, l, 0)
+        red_z(1, l, *ORDER[:2])
+        red_sum(4, l)
+        red_z(1, l, *last)
+        red_z(1, l, 0)
+        if first:
+            red_z(2, 1)
+            red_sum(3, 1)
+
+    red_z(5, 0)
+    red_z(2, 0)
     red_sum(3, 0)
-    red_sum(2, 0)
-    red_z(1, 0)
-    red_z(5, 0)
-    red_write(3, 0)
-    red_write(2, 0)
     red_sum(1, 0)
     red_sum(5, 0)
+    red_write(3, 0)
+    red_sum(2, 0)
     red_write(1, 0)
     red_write(5, 0)
+    red_write(2, 0)
     flush()
     for g, i in sent_weights:
-        part = W[g].at[0, 0:CH]
-        rc(part, part, x_peer, i).wait_send()
+        ref = W[g].at[0, part(g, 0)]
+        rc(ref, ref, x_peer, i).wait_send()
 
 
 def fused_step(inputs, cotangent, image_lengths, attention, upward, downward, vectors, bias_up):
@@ -1110,24 +1231,25 @@
     widths = {1: 640, 2: D, 3: D, 4: D, 5: 128}
     scratch = [
         V((L, D, 640), BF16), V((L, D, D), BF16), V((L, D, D), BF16), V((L, D, D), BF16),
-        V((3 * T, D), BF16),
+        V((4 * T, D), BF16),
         V((6, T, D), BF16),
         V((L, N, D), BF16), V((L, N, D), BF16), V((L, N, D), BF16),
         V((L, 3, N, 128), BF16), V((L, 2, N, 128), BF16), V((L, 2, N, 128), BF16),
         V((L, 2, 128, N), BF16), V((2, 128, N), BF16),
         V((L, N, 256), BF16), V((L, T, D), BF16),
-        V((N, 256), BF16), V((S, T, 256), BF16), V((T, D), BF16),
+        V((N, 256), BF16), V((T, D), BF16),
         V((L, 8, N), F32),
-        V((L, T, D), F32), V((T, D), F32),
+        V((L, T, D), F32), V((T, D), F32), V((T, D), F32),
         V((L, N, D), BF16), V((L, N, D), BF16),
         V((N, 128), jnp.int32), V((8, N), jnp.int32),
         V((N, D), F32),
         V((N, 640), BF16),
         *[V((D, widths[g]), BF16) for g in range(1, 6)],
-        *[V((NZ, CH, widths[g]), BF16) for g in range(1, 6)],
-        *[V((NZ - 1, CH, widths[g]), BF16) for g in range(1, 6)],
-        *[V((S, RP, widths[g]), BF16) for g in (1, 2, 3, 5)],
-        *[V((S, RP, widths[g]), BF16) for g in (1, 2, 3, 5)],
+        *[V((NZ, CH // 2 if g == 2 else CH, widths[g]), BF16) for g in range(1, 6)],
+        *[V((NZ - 1, CH // 2 if g == 2 else CH, widths[g]), BF16) for g in range(1, 6)],
+        V((DP, CH // 2, D), BF16),
+        *[V((2 if g == 2 else S, RP, widths[g]), BF16) for g in (1, 2, 3, 5)],
+        *[V((2 if g == 2 else S, RP, widths[g]), BF16) for g in (1, 2, 3, 5)],
         V((128, 128), F32), V((32, D), F32), V((128, D), F32),
         pltpu.SemaphoreType.DMA((SEMS,)), pltpu.SemaphoreType.DMA((SEMS,)),
         pltpu.SemaphoreType.REGULAR((8,)), pltpu.SemaphoreType.REGULAR((8,)),
@@ -1163,6 +1285,45 @@
         and upward.shape[2] == seq_count * width
         and bias_up.shape[1] % 16 == 0
     )
+
+
+def update_kernel(rate, *refs):
+    for member in range(5):
+        gradient, master, moment, average = (refs[5 * k + member][...] for k in range(4))
+        results = optimizer_step(gradient, master, moment, average, rate)
+        for k in range(5):
+            refs[22 + 5 * member + k][...] = results[k]
+    for k in range(2):
+        refs[47 + k][...] = refs[20 + k][...]
+
+
+def fused_update(rate, output, input_grad, reduced, masters, moments, averages):
+    attention, upward, downward, vectors, bias_up = masters
+    halves = [
+        pl.BlockSpec((1, 2) + attention.shape[2:], lambda l, i: (l, i, 0, 0)),
+        pl.BlockSpec((1, upward.shape[1], upward.shape[2] // 2), lambda l, i: (l, 0, i)),
+        pl.BlockSpec((1, downward.shape[1] // 2, downward.shape[2]), lambda l, i: (l, i, 0)),
+        pl.BlockSpec((1,) + vectors.shape[1:], lambda l, i: (l, 0, 0)),
+        pl.BlockSpec(bias_up.shape, lambda l, i: (0, 0)),
+    ]
+    tokens = pl.BlockSpec(
+        (1, output.shape[1] // 4, output.shape[2]), lambda l, i: (0, 2 * l + i, 0)
+    )
+    outs, specs = [], []
+    for member in range(5):
+        for k in range(5):
+            outs.append(jax.ShapeDtypeStruct(masters[member].shape, BF16 if k == 4 else F32))
+            specs.append(halves[member])
+    outs += [jax.ShapeDtypeStruct(output.shape, BF16)] * 2
+    results = pl.pallas_call(
+        functools.partial(update_kernel, rate),
+        grid=(2, 2),
+        out_shape=outs,
+        in_specs=halves * 4 + [tokens] * 2,
+        out_specs=specs + [tokens] * 2,
+        compiler_params=pltpu.CompilerParams(vmem_limit_bytes=VMEM_BYTES),
+    )(*reduced, *masters, *moments, *averages, output, input_grad)
+    return tuple(results[25:]) + tuple(results[:25])
 
 
 def per_device(
@@ -1190,6 +1351,10 @@
     seq_count = lax.axis_size("seq")
     if fits_fused(inputs, attention_weight, up_weight, hidden_bias, dp_count, seq_count):
         output, input_grad, *reduced = fused_step(inputs, cotangent, image_lengths, *masters)
+        moments = (attention_moment, up_moment, down_moment, vector_moment, bias_moment)
+        averages = (attention_average, up_average, down_average, vector_average, bias_average)
+        rate = LEARN_BASE / math.sqrt(inputs.shape[0] * inputs.shape[1] * dp_count * seq_count)
+        return fused_update(rate, output, input_grad, reduced, masters, moments, averages)
     else:
         output, input_grad, *reduced = plain_step(inputs, cotangent, image_lengths, masters)
     total_tokens = inputs.shape[0] * inputs.shape[1] * dp_count * seq_count

time: 344 us -> 254 us (0.74)
  Pallas kernels: 322 us -> 253 us
  other arithmetic: 9.72 us -> 0 us
  local copies, waits for them, and re-layouts: 9.5 us -> 0 us
    pallas_call x1, Pallas kernels: 322 us -> 246 us  [fused_step(): pl.pallas_call(functools.partial(step_kernel, NZ), out_shape=(jax.ShapeDt...]
    unnamed x57 -> x0, local copies, waits for them, and re-layouts: 9.5 us -> none
    pallas_call x0 -> x1, Pallas kernels: none -> 7.58 us  [fused_update(): pl.pallas_call(functools.partial(update_kernel, rate), grid=(2, 2), out_s...]
    convert_element_type x5 -> x0, other arithmetic: 5.92 us -> none  [optimizer_step(): master_new.astype(jnp.bfloat16)]
    add x5 -> x0, other arithmetic: 3.81 us -> none  [optimizer_step(): average_new = AVERAGE_RATE * average + (1.0 - AVERAGE_RATE) * master_new]
where the time goes in v2:
time: 254 us
  Pallas kernels  253 us (100%)
    pallas_call x1, Pallas kernels, fused_step(): pl.pallas_call(functools.partial(step_kernel, NZ), out_shape=(jax.ShapeDt...  246 us
    pallas_call x1, Pallas kernels, fused_update(): pl.pallas_call(functools.partial(update_kernel, rate), grid=(2, 2), out_s...  7.58 us

profile of v2, /device:TPU:0, one launch (start us, length us, event | category | flops | bytes accessed | tf_op | source)
XLA Modules:
  0.0 254.1 jit_solution(11809492913571455572)
XLA Ops:
  0.7 245.7 %shard_map.385 = (bf16[1,256,768]{2,1,0:T(8,128)(2,1)}, bf16[1,256,768]{2,1,0:T(8,128)(2,1)}, f32[2,4,24,768]{3,2,1,0:T(8,128)}, f32[2,24,3072]{2,1,0:T(8,128)},...) custom-call(bf16[1,256,768]{2,1,0:T(8,128)(2,1)} %x_in.1, bf16[1,256,768]{2,1,0:T(8,128)(2,1)} %cot_in.1, ...), custom_call_target="tpu_custom_call" | custom-call | tf_op jit(solution)/shard_map/pallas_call | solution.py:1257
  246.3 7.6 %shard_map.386 = (f32[2,4,24,768]{3,2,1,0:T(8,128)}, f32[2,4,24,768]{3,2,1,0:T(8,128)}, f32[2,4,24,768]{3,2,1,0:T(8,128)}, f32[2,4,24,768]{3,2,1,0:T(8,128)}, bf...) custom-call(f32[2,4,24,768]{3,2,1,0:T(8,128)} %get-tuple-element.61., ...), custom_call_target="tpu_custom_call" | custom-call | tf_op jit(solution)/shard_map/pallas_call | solution.py:1318
